TPU v7x, 128 devices: a whole 4x4x4 slice. The times are simulated.
128 devices in a mesh: pts: 64 (over z, y, x), grp: 2 (over core).
Axes of the slice: x: 4, y: 4, z: 4, core: 2. Of those that a mesh axis runs over, the one named last changes fastest.
Arguments:
- points: bfloat16 [131072, 256], P('pts'), may hold values from -6 to 6
- neighbours: int32 [131072, 27], P('pts'), may hold values from -1 to 131071, as said below
- patch_len: int32 [256], replicated, may hold values from 1 to 1024, as said below
- zorder: int32 [131072], P('pts'), may hold values from 0 to 131071, as said below
- conv_w: bfloat16 [27, 256, 256], P(None, None, 'grp'), may hold values from -0.078125 to 0.078125
- conv_b: float32 [256], P('grp'), may hold values from -3 to 3
- cpe_w: bfloat16 [256, 256], replicated, may hold values from -0.375 to 0.375
- cpe_b: float32 [256], replicated, may hold values from -3 to 3
- cpe_gain: float32 [256], replicated, may hold values from 0.1 to 1.9
- norm1_gain: float32 [256], replicated, may hold values from 0.1 to 1.9
- qkv_w: bfloat16 [256, 3, 256], P(None, None, 'grp'), may hold values from -2 to 2
- qkv_b: float32 [3, 256], P(None, 'grp'), may hold values from -3 to 3
- proj_w: bfloat16 [256, 256], replicated, may hold values from -0.375 to 0.375
- proj_b: float32 [256], replicated, may hold values from -3 to 3
- norm2_gain: float32 [256], replicated, may hold values from 0.1 to 1.9
- fc1_w: bfloat16 [256, 1024], P(None, 'grp'), may hold values from -0.375 to 0.375
- fc1_b: float32 [1024], P('grp'), may hold values from -3 to 3
- fc2_w: bfloat16 [1024, 256], P('grp'), may hold values from -0.1875 to 0.1875
- fc2_b: float32 [256], replicated, may hold values from -3 to 3
Outputs:
- next_rows: bfloat16 [131072, 256], P('pts')
Inputs may be any that keep to these rules, and one draw needn't show every extreme that they name: `neighbours`: tap 13 is the row itself; every other entry is -1 or a row at most 256 rows away; rows at exactly 256 away on both sides occur. `zorder`: A permutation. The rows of next_rows on one device come in runs of 64; each run is a whole aligned run of 64 rows of one source device, in one common inner order, and the 64-row runs of one device come from 32 different source devices at relative offsets (mod 64) common to all devices, one of which is 32. `patch_len`: patches sum to 131072 rows, one has exactly 1024.
All inputs are finite; a program needn't handle non-finite values.
Results may differ from a plain program's by a relative error of at most 0.022.
Values may be sent and summed in bfloat16 or wider, within the bound.
No kernel may reach another device: no remote copies, remote signals or barrier semaphores. Data moves between devices by JAX's collectives and lax.ppermute only.
A program may use at most 128 MiB of HBM per device.

v0:
```python
import jax
import jax.numpy as jnp
from jax import lax
from jax.experimental import pallas as pl
from jax.experimental.pallas import tpu as pltpu
from jax.sharding import PartitionSpec as P

F32=jnp.float32; BF=jnp.bfloat16

VMEM_BYTES = 64 * 2**20 - 65536
Q_SCALE = 0.25 * 1.4426950408889634


def layer_norm(v, gain):
    c = v - jnp.mean(v, axis=-1, keepdims=True)
    s = jnp.mean(c * c, axis=-1, keepdims=True)
    return c * lax.rsqrt(s + 1e-05) * gain

RB = 128
TAPS = [t for t in range(27) if t != 13]


def copies(sems, pairs):
    out = [pltpu.make_async_copy(src, dst, sems.at[i]) for i, (src, dst) in enumerate(pairs)]
    for copy in out:
        copy.start()
    return out


def wait(some):
    for copy in some:
        copy.wait()


def turned(ref, g):
    first = ref.at[pl.ds(pl.multiple_of(128 * g, 128), 128)]
    return first, ref.at[pl.ds(pl.multiple_of(128 - 128 * g, 128), 128)]


def conv_kernel(
    sc, pts, low, high, nbs, wm, wo, cbm, cbo, cpw, cpb, cpg, n1g, sec_o, nrm_o, lo_o, hi_o,
    X, NT, NB, OH, G, W, CW, CB, CV, sems,
):
    g = sc[0]
    base = sc[1]
    cw_a, cw_b = turned(cpw, g)
    started = copies(
        sems,
        [
            (nbs, NT), (pts, X.at[256:2304]), (low, X.at[0:256]), (high, X.at[2304:2560]),
            (wm, W.at[:, 0:128]), (wo, W.at[:, 128:256]), (cw_a, CW.at[0:128]),
            (cw_b, CW.at[128:256]), (cbm, CB.at[:, 0:128]), (cbo, CB.at[:, 128:256]),
            (cpb, CV.at[0]), (cpg, CV.at[1]), (n1g, CV.at[2]),
        ],
    )
    wait(started[:4])
    lanes = lax.broadcasted_iota(jnp.int32, (RB, 768), 1)
    for b in range(8):
        NB[256 * b : 256 * b + 256, :] = jnp.transpose(NT[:, 256 * b : 256 * b + 256])

    def block(b, OH):
        rel = []
        for j in range(RB // 32):
            rel.append(NB[pl.ds(pl.multiple_of(256 * b + 64 * j + 32 * g, 32), 32), :])
        rel = jnp.concatenate(rel, axis=0)
        rel = jnp.where(rel < 0, -1, rel - (base + 256 * b - 256))
        for i, t in enumerate(TAPS):
            col = rel[:, t : t + 1]
            OH[i * RB : (i + 1) * RB, :] = jnp.where(
                lanes == col, jnp.array(1, BF), jnp.array(0, BF)
            )
        win = X[pl.ds(256 * b, 768), :]
        to = pl.ds(b * RB, RB)
        out = jnp.dot(OH[...], win, preferred_element_type=F32).astype(BF)
        for i, t in enumerate(TAPS):
            G[to, t * 256 : (t + 1) * 256] = out[i * RB : (i + 1) * RB, :]
        for j in range(RB // 32):
            G[pl.ds(b * RB + 32 * j, 32), 13 * 256 : 14 * 256] = X[
                pl.ds(pl.multiple_of(256 + 256 * b + 64 * j + 32 * g, 32), 32), :
            ]

    for b in range(1024 // RB):
        block(b, OH.at[b % 2])
    wait(started[4:])

    def finish(m, _):
        r0 = pl.multiple_of(m * 512, 512)
        at = pl.ds(r0, 512)
        acc = jnp.dot(G[at, :], W[...], preferred_element_type=F32)
        conv = (acc + CB[...]).astype(BF)
        c = jnp.dot(conv, CW[...], preferred_element_type=F32) + CV[0]
        own = G[at, 13 * 256 : 14 * 256].astype(F32)
        sec = (own + layer_norm(c, CV[1])).astype(BF)
        sec_o[at, :] = sec
        normed = layer_norm(sec.astype(F32), CV[2]).astype(BF)
        nrm_o[at, :] = normed

        @pl.when(m == 0)
        def _():
            hi_o[...] = normed

        @pl.when(m == 1)
        def _():
            lo_o[...] = normed

        return 0

    lax.fori_loop(0, 2, finish, 0)


def call(kernel, name, smem, args, out_shape, scratch, sems, flops, space=pltpu.VMEM):
    return pl.pallas_call(
        kernel,
        out_shape=out_shape,
        in_specs=[pl.BlockSpec(memory_space=pltpu.SMEM)] * smem
        + [pl.BlockSpec(memory_space=pltpu.HBM)] * (len(args) - smem),
        out_specs=[pl.BlockSpec(memory_space=space)] * len(out_shape),
        scratch_shapes=[pltpu.VMEM(*x) for x in scratch] + [pltpu.SemaphoreType.DMA((sems,))],
        compiler_params=pltpu.CompilerParams(vmem_limit_bytes=VMEM_BYTES),
        cost_estimate=pl.CostEstimate(flops=flops, bytes_accessed=8 * 10**6, transcendentals=0),
        name=name,
    )(*args)


def conv_call(*args):
    out = [jax.ShapeDtypeStruct((n, 256), BF) for n in (1024, 1024, 512, 512)]
    scratch = [
        ((2560, 256), BF), ((27, 2048), jnp.int32), ((2048, 27), jnp.int32), ((2, 26 * RB, 768), BF), ((1024, 6912), BF),
        ((6912, 256), BF), ((256, 256), BF), ((1, 256), F32), ((3, 1, 256), F32),
    ]
    return call(conv_kernel, "conv", 1, args, out, scratch, 13, 30 * 10**9)


def key_values(NE, KT, V, QW, QB):
    wkt = [jnp.transpose(QW[h, 1]) for h in range(2)]
    bkc = [jnp.transpose(jnp.broadcast_to(QB[h, 1:2, :], (8, 128)))[:, :1] for h in range(2)]
    wv = jnp.concatenate([QW[0, 2], QW[1, 2]], axis=1)
    bv = jnp.concatenate([QB[0, 2:3, :], QB[1, 2:3, :]], axis=1)

    def block(i, most):
        r0 = pl.multiple_of(i * 256, 256)
        rows = NE[pl.ds(4 * i, 4)].reshape(256, 256)
        for h in range(2):
            kt = (
                lax.dot_general(
                    wkt[h], rows, (((1,), (1,)), ((), ())), preferred_element_type=F32
                )
                + bkc[h]
            )
            most = jnp.maximum(most, jnp.sum((kt * kt).reshape(8, 16, 256), axis=1))
            KT[128 * h : 128 * h + 128, pl.ds(r0, 256)] = kt.astype(BF)
        V[pl.ds(r0, 256), :] = (jnp.dot(rows, wv, preferred_element_type=F32) + bv).astype(BF)
        return most

    return block


def patch_rows(plen):
    lens = jnp.broadcast_to(plen.astype(F32), (256, 256))
    sub = lax.broadcasted_iota(jnp.int32, (256, 256), 0)
    lane = lax.broadcasted_iota(jnp.int32, (256, 256), 1)
    ends_col = jnp.sum(jnp.where(lane <= sub, lens, 0.0), axis=1, keepdims=True)
    ends_row = jnp.sum(jnp.where(lane == sub, ends_col, 0.0), axis=0, keepdims=True)
    return ends_row - plen.astype(F32), ends_row


def limits(qb, g, base, total, starts_row, ends_row):
    r = lax.broadcasted_iota(jnp.int32, (256, 1), 0)
    row = (base + 512 * qb + 64 * (r // 32) + 32 * g + r % 32).astype(F32)
    first = jnp.max(jnp.where(starts_row <= row, starts_row, 0.0), axis=1, keepdims=True)
    finish = jnp.min(jnp.where(ends_row > row, ends_row, total.astype(F32)), axis=1, keepdims=True)
    shift = (1024 - base).astype(F32)
    first = (first + shift).astype(jnp.int32)
    finish = (finish + shift).astype(jnp.int32)
    kb0 = jnp.maximum(jnp.min(first) // 128, 0)
    kb1 = jnp.minimum((jnp.max(finish) + 127) // 128, 32)
    return first, finish, kb0, kb1


def queries(rows, QW, QB):
    wq = jnp.concatenate([QW[0, 0], QW[1, 0]], axis=1)
    bq = jnp.concatenate([QB[0, 0:1, :], QB[1, 0:1, :]], axis=1)
    return ((jnp.dot(rows, wq, preferred_element_type=F32) + bq) * Q_SCALE).astype(BF)


def pair_tools():
    half = lax.broadcasted_iota(jnp.int32, (32, 128), 0) < 16
    k_low = jnp.where(half, 1.0, 0.0).astype(BF)
    k_high = jnp.where(half, 0.0, 1.0).astype(BF)
    col_head = lax.broadcasted_iota(jnp.int32, (128, 128), 1) // 16
    cols = [jnp.where(col_head == a, 1.0, 0.0).astype(BF) for a in range(8)]

    def mask(kb, first, finish):
        key = kb * 128 + lax.broadcasted_iota(jnp.int32, (256, 128), 1)
        madd = jnp.where((key >= first) & (key < finish), 0.0, -jnp.inf)
        return jnp.concatenate([madd, madd], axis=1)

    def scores(Q8, p, kt, madd):
        part = kt[32 * p : 32 * p + 32, :]
        pair = jnp.concatenate([part * k_low, part * k_high], axis=1)
        return jnp.dot(Q8[p], pair, preferred_element_type=F32) + madd

    def step(kb, k0, Q8, KT, V, first, finish, M=None):
        kt = KT[:, pl.ds(k0, 128)]
        vb = V[pl.ds(k0, 128), :]
        madd = mask(kb, first, finish)
        out = []
        for h in range(2):
            vh = vb[:, 128 * h : 128 * h + 128]
            ps, vs = [], []
            for a in range(4):
                p = 4 * h + a
                s = scores(Q8, p, kt, madd)
                if M is not None:
                    s = s - M[p]
                ps.append(jnp.exp2(s).astype(BF))
                for c in (cols[2 * a], cols[2 * a + 1]):
                    vs.append(jnp.concatenate([vh * c, c], axis=1))
            out.append(
                jnp.dot(
                    jnp.concatenate(ps, axis=1),
                    jnp.concatenate(vs, axis=0),
                    preferred_element_type=F32,
                )
            )
        return out

    return mask, scores, step


def near_kernel(
    sc, plen, own, oth, qkvm, qkvo, qbm, qbo, acc_h, q_h, most_h, NE, KT, V, Q8, acc_o, q_o,
    most_o, QW, QB, PL, sems,
):
    g, base, total = sc[0], sc[1], sc[2]
    wait(
        copies(
            sems,
            [
                (own, NE.at[:, g]), (oth, NE.at[:, 1 - g]), (qkvm, QW.at[0]), (qkvo, QW.at[1]),
                (qbm, QB.at[0]), (qbo, QB.at[1]), (plen, PL),
            ],
        )
    )
    block = key_values(NE, KT, V, QW, QB)
    most = lax.fori_loop(0, 8, block, jnp.zeros((8, 256), F32))
    most_o[...] = jnp.broadcast_to(jnp.max(most), (8, 128))
    leave = pltpu.make_async_copy(most_o, most_h, sems.at[7])
    leave.start()

    def results(qb):
        at = pl.ds(pl.multiple_of(256 * qb, 256), 256)
        return (
            pltpu.make_async_copy(acc_o.at[qb], acc_h.at[qb], sems.at[8 + qb]),
            pltpu.make_async_copy(q_o.at[at], q_h.at[at], sems.at[12 + qb]),
        )

    starts_row, ends_row = patch_rows(PL[...])
    mask, scores, step = pair_tools()

    def q_block(qb, _):
        r0 = pl.multiple_of(qb * 256, 256)
        q = queries(NE[pl.ds(8 * qb, 8), g].reshape(256, 256), QW, QB)
        q_o[pl.ds(r0, 256), :] = q
        for p in range(8):
            Q8[p] = q[:, 32 * p : 32 * p + 32]
        first, finish, kb0, kb1 = limits(qb, g, base, total, starts_row, ends_row)
        acc_o[qb] = jnp.zeros((2, 256, 256), F32)

        def body(kb, _):
            k0 = pl.multiple_of((kb - 8) * 128, 128)
            for h, x in enumerate(step(kb, k0, Q8, KT, V, first, finish)):
                acc_o[qb, h] += x
            return 0

        lax.fori_loop(jnp.maximum(kb0, 8), jnp.minimum(kb1, 24), body, 0)
        for copy in results(qb):
            copy.start()
        return 0

    lax.fori_loop(0, 4, q_block, 0)
    leave.wait()
    for qb in range(4):
        wait(results(qb))


QKV_SCRATCH = [((2, 3, 256, 128), BF), ((2, 3, 128), F32), ((1, 256), jnp.int32)]


def near_call(*args):
    out = [
        jax.ShapeDtypeStruct((4, 2, 256, 256), F32),
        jax.ShapeDtypeStruct((1024, 256), BF),
        jax.ShapeDtypeStruct((8, 128), F32),
    ]
    scratch = [
        ((32, 2, 32, 256), BF), ((256, 2048), BF), ((2048, 256), BF), ((8, 256, 32), BF),
        ((4, 2, 256, 256), F32), ((1024, 256), BF), ((8, 128), F32),
    ] + QKV_SCRATCH
    return call(near_kernel, "near", 1, args, out, scratch, 16, 20 * 10**9, space=pltpu.HBM)


def far_kernel(
    sc, sel, plen, own, oth, lo_own, lo_oth, hi_own, hi_oth, sec_i, acc_i, q_i, most_i, qkvm, qkvo,
    qbm, qbo, prw, prb, n2g, f1m, f1o, b1m, b1o, f2m, f2o, f2b, send, NE, KT, V, Q8, ACC, OUT, M,
    SEC, AI, QI, MI, PW, VEC, F1, B1, F2, QW, QB, PL, sems,
):
    g, base, total = sc[0], sc[1], sc[2]
    pw_a, pw_b = turned(prw, g)
    started = copies(
        sems,
        [
            (lo_own, NE.at[0:16, g]), (lo_oth, NE.at[0:16, 1 - g]), (hi_own, NE.at[48:64, g]),
            (hi_oth, NE.at[48:64, 1 - g]), (qkvm, QW.at[0]), (qkvo, QW.at[1]), (qbm, QB.at[0]),
            (qbo, QB.at[1]), (plen, PL), (most_i, MI), (q_i, QI), (acc_i, AI), (sec_i, SEC),
            (pw_a, PW.at[0:128]), (pw_b, PW.at[128:256]), (prb, VEC.at[0]), (n2g, VEC.at[1]),
            (f2b, VEC.at[2]), (f1m, F1.at[0]), (f1o, F1.at[1]), (b1m, B1.at[0]), (b1o, B1.at[1]),
            (f2m, F2.at[0]), (f2o, F2.at[1]),
        ],
    )
    wait(started[:11])
    block = key_values(NE, KT, V, QW, QB)
    starts_row, ends_row = patch_rows(PL[...])
    edge_lo = limits(0, g, base, total, starts_row, ends_row)[2]
    edge_hi = limits(3, g, base, total, starts_row, ends_row)[3]
    most = lax.fori_loop(jnp.minimum(edge_lo // 2, 4), 4, block, jnp.zeros((8, 256), F32))
    most = lax.fori_loop(12, jnp.maximum((edge_hi + 1) // 2, 12), block, most)
    key_most = jnp.maximum(jnp.max(most), jnp.max(MI[...]))
    mask, scores, step = pair_tools()
    hs = lax.broadcasted_iota(jnp.int32, (256, 128), 0) // 16
    hl = lax.broadcasted_iota(jnp.int32, (256, 128), 1)
    head_sel = jnp.where(hs == hl, 1.0, 0.0).astype(BF)
    def q_most(r0):
        q = QI[pl.ds(r0, 256), :]
        return jnp.max(jnp.dot(q * q, head_sel, preferred_element_type=F32))

    bound = q_most(0)
    for i in range(1, 4):
        bound = jnp.maximum(bound, q_most(256 * i))
    calm = bound * key_most * 1.05 <= 1e4

    @pl.when(jnp.logical_not(calm))
    def _():
        wait(copies(sems.at[24:26], [(own, NE.at[16:48, g]), (oth, NE.at[16:48, 1 - g])]))
        lax.fori_loop(4, 12, block, jnp.zeros((8, 256), F32))

    wait(started[11:])

    def q_block(qb, _):
        r0 = pl.multiple_of(qb * 256, 256)
        q = QI[pl.ds(r0, 256), :]
        for p in range(8):
            Q8[p] = q[:, 32 * p : 32 * p + 32]
        first, finish, kb0, kb1 = limits(qb, g, base, total, starts_row, ends_row)

        def body(kb, _, M=None):
            k0 = pl.multiple_of(kb * 128, 128)
            for h, x in enumerate(step(kb, k0, Q8, KT, V, first, finish, M)):
                ACC[h] += x
            return 0

        @pl.when(calm)
        def _():
            ACC[...] = AI[qb]
            lax.fori_loop(kb0, jnp.minimum(kb1, 8), body, 0)
            lax.fori_loop(jnp.maximum(kb0, 24), kb1, body, 0)

        @pl.when(jnp.logical_not(calm))
        def _():
            ACC[...] = jnp.zeros_like(ACC)
            M[...] = jnp.full(M.shape, -jnp.inf, F32)

            def top(kb, _):
                kt = KT[:, pl.ds(pl.multiple_of(kb * 128, 128), 128)]
                madd = mask(kb, first, finish)
                for p in range(8):
                    M[p] = jnp.maximum(M[p], scores(Q8, p, kt, madd))
                return 0

            lax.fori_loop(kb0, kb1, top, 0)
            for p in range(8):
                for h in range(2):
                    part = M[p, :, 128 * h : 128 * h + 128]
                    M[p, :, 128 * h : 128 * h + 128] = jnp.broadcast_to(
                        jnp.max(part, axis=1, keepdims=True), (256, 128)
                    )
            lax.fori_loop(kb0, kb1, lambda kb, c: body(kb, c, M), 0)

        attn = jnp.concatenate(
            [ACC[h, :, 0:128] / ACC[h, :, 128:256] for h in range(2)], axis=1
        ).astype(BF)
        two = (
            SEC[pl.ds(r0, 256), :].astype(F32)
            + jnp.dot(attn, PW[...], preferred_element_type=F32)
            + VEC[0]
        ).astype(BF)
        wide = two.astype(F32)
        normed = layer_norm(wide, VEC[1]).astype(BF)
        total_rows = wide + VEC[2]
        for h in range(2):
            x = jnp.dot(normed, F1[h], preferred_element_type=F32) + B1[h]
            x = (0.5 * x * (1.0 + lax.erf(x * 0.7071067811865476))).astype(BF)
            total_rows = total_rows + jnp.dot(x, F2[h], preferred_element_type=F32)
        OUT[pl.ds(r0, 256), :] = total_rows.astype(BF)
        return 0

    lax.fori_loop(0, 4, q_block, 0)

    def place(d, _):
        send[pl.ds(pl.multiple_of(32 * d, 32), 32), :] = OUT[
            pl.ds(pl.multiple_of(32 * sel[d], 32), 32), :
        ]
        return 0

    lax.fori_loop(0, 64, place, 0, unroll=4)


def far_call(*args):
    scratch = [
        ((64, 2, 32, 256), BF), ((256, 4096), BF), ((4096, 256), BF), ((8, 256, 32), BF),
        ((2, 256, 256), F32), ((1024, 256), BF), ((8, 256, 256), F32), ((1024, 256), BF),
        ((4, 2, 256, 256), F32), ((1024, 256), BF), ((8, 128), F32), ((256, 256), BF),
        ((3, 1, 256), F32), ((2, 256, 512), BF), ((2, 1, 512), F32), ((2, 512, 256), BF),
    ] + QKV_SCRATCH
    out = [jax.ShapeDtypeStruct((2048, 256), BF)]
    return call(far_kernel, "far", 2, args, out, scratch, 26, 20 * 10**9)[0]


def last_kernel(sc, zs, zv, own, oth, out):
    g = sc[0]
    place = zv[0:1, 0:64] % 64
    place = place % 32 + jnp.where(place // 32 == g, 0, 32)
    place = jnp.where(lax.broadcasted_iota(jnp.int32, (64, 64), 0) == place, 1.0, 0.0)
    perm = jnp.transpose(place).astype(BF)

    def step(k, _):
        source = lax.shift_right_logical(zs[64 * k], 11)
        rows = jnp.concatenate([own[source], oth[source]], axis=0)
        out[pl.ds(pl.multiple_of(64 * k, 64), 64), :] = jnp.dot(
            perm, rows, preferred_element_type=F32
        ).astype(BF)
        return 0

    lax.fori_loop(0, 32, step, 0, unroll=8)


def last_call(*args):
    smem, vmem = pl.BlockSpec(memory_space=pltpu.SMEM), pl.BlockSpec(memory_space=pltpu.VMEM)
    return pl.pallas_call(
        last_kernel,
        out_shape=jax.ShapeDtypeStruct((2048, 256), BF),
        in_specs=[smem] * 2 + [vmem] * 3,
        out_specs=vmem,
        compiler_params=pltpu.CompilerParams(vmem_limit_bytes=16 * 2**20),
        name="relabel",
    )(*args)


def local(
    points, neighbours, patch_len, zorder, conv_w, conv_b, cpe_w, cpe_b, cpe_gain, norm1_gain,
    qkv_w, qkv_b, proj_w, proj_b, norm2_gain, fc1_w, fc1_b, fc2_w, fc2_b,
):
    g = lax.axis_index("grp").astype(jnp.int32)
    me = lax.axis_index("pts").astype(jnp.int32)
    peers = lax.axis_size("pts")
    rows = points.shape[0]
    forward = [(i, i + 1) for i in range(peers - 1)]
    backward = [(i + 1, i) for i in range(peers - 1)]

    def swap(x):
        return lax.ppermute(x, "grp", [(0, 1), (1, 0)])

    def pieces(x):
        return x.reshape(-1, 32, 256)

    order = zorder.reshape(16, 128)
    low = lax.ppermute(points[rows - 256 :], "pts", forward)
    high = lax.ppermute(points[:256], "pts", backward)
    sources = jnp.arange(peers, dtype=jnp.int32)[:, None]
    run = zorder[::64][None, :]
    wanted = jnp.max(jnp.where(run // rows == sources, run % rows // 64, 0), axis=1)
    wanted = jnp.broadcast_to(wanted[:, None, None], (peers, 1, 128))
    sel = lax.all_to_all(wanted, "pts", split_axis=0, concat_axis=0, tiled=True)[:, 0, 0]
    sel, low = lax.optimization_barrier((sel, low))
    conv_m = conv_w.reshape(27 * 256, 128)
    conv_o, bias_o = swap(conv_m), swap(conv_b)
    scalars = jnp.stack([g, me * rows, jnp.int32(rows * peers)])
    section_one, normed, lo_half, hi_half = conv_call(
        scalars, points, low, high, neighbours.T, conv_m, conv_o, conv_b[None], bias_o[None],
        cpe_w, cpe_b[None], cpe_gain[None], norm1_gain[None],
    )
    qkv_m = jnp.transpose(qkv_w, (1, 0, 2))
    weights = (qkv_m, swap(qkv_m), qkv_b, swap(qkv_b))
    fc1_o, fc2_o, b1_o = swap(fc1_w), swap(fc2_w), swap(fc1_b)
    other = swap(normed)
    lo_own = lax.ppermute(lo_half, "pts", forward)
    hi_own = lax.ppermute(hi_half, "pts", backward)
    acc, query, most = near_call(scalars, patch_len[None], pieces(normed), pieces(other), *weights)
    lo_own, hi_own, most = lax.optimization_barrier((lo_own, hi_own, most))
    lo_oth, hi_oth = swap(lo_own), swap(hi_own)
    send = far_call(
        scalars, sel, patch_len[None], pieces(normed), pieces(other), pieces(lo_own),
        pieces(lo_oth), pieces(hi_own), pieces(hi_oth), section_one, acc, query, most, *weights,
        proj_w, proj_b[None], norm2_gain[None], fc1_w, fc1_o, fc1_b[None], b1_o[None], fc2_w,
        fc2_o, fc2_b[None],
    )
    got = lax.all_to_all(send, "pts", split_axis=0, concat_axis=0, tiled=True)
    return last_call(scalars, zorder, order, pieces(got), pieces(swap(got)))


def solution(mesh):
    placed = (
        P("pts", None), P("pts", None), P(), P("pts"), P(None, None, "grp"), P("grp"), P(), P(), P(),
        P(), P(None, None, "grp"), P(None, "grp"), P(), P(), P(), P(None, "grp"), P("grp"),
        P("grp", None), P(),
    )
    return jax.shard_map(
        local, mesh=mesh, in_specs=placed, out_specs=P("pts", None), check_vma=False
    )
```

profile of v0, /device:TPU:1, one launch (start us, length us, event | category | flops | bytes accessed | tf_op | source)
XLA Modules:
  0.0 176.2 jit_solution(4888899463467708891)
XLA Ops:
  0.0 1.4 collective-permute-start.2
  1.4 0.8 slice.12
  2.3 0.1 select_reduce_fusion
  2.3 0.8 broadcast_in_dim.56
  3.1 11.2 %all-to-all-start = ((s32[64,1,128]{2,1,0:T(1,128)}), s32[64,1,128]{2,1,0:T(1,128)S(1)}, u32[]{:S(2)}, u32[]{:S(2)}) async-start(s32[64,1,128]{2,1,0:T(1,128)} %broadcast_in_dim.56), calls=%async_computation | async-start | bytes 65536 | tf_op jit(solution)/shard_map/all_to_all | solution.py:483
  14.3 1.0 fusion
  15.3 1.3 collective-permute-start.1
  16.6 4.0 %collective-permute-start = (bf16[256,256]{1,0:T(8,128)(2,1)S(1)}, bf16[256,256]{1,0:T(8,128)(2,1)S(1)}, u32[]{:S(2)}, u32[]{:S(2)}) collective-permute-start(bf16[256,256]{1,0:T(8,128)(2,1)S(1)} %get-tuple-element.30), channel_id=1, source_target_pairs={{0,2},{2,4},{4,6},{6,8},{8,10},{10,12},{12,14},{14,16},{16,18},{18... | collective-permute-start | bytes 393224 | tf_op jit(solution)/shard_map/ppermute | solution.py:477
  20.6 0.6 pad_add_fusion.sc
  21.2 1.4 all-to-all-done
  22.7 1.9 %slice_reduce_fusion.sel = s32[64]{0:T(128)} fusion(s32[64,1,128]{2,1,0:T(1,128)S(1)} %all-to-all-done), kind=kLoop, calls=%fused_computation | loop fusion | bytes 512 | tf_op jit(solution)/shard_map/slice | solution.py:483
  24.5 0.7 copy-done.2
  25.3 20.4 %conv.1 = (bf16[1024,256]{1,0:T(8,128)(2,1)}, bf16[1024,256]{1,0:T(8,128)(2,1)}, bf16[512,256]{1,0:T(8,128)(2,1)}, bf16[512,256]{1,0:T(8,128)(2,1)}) custom-call(s32[3]{0:T(128)} %pad_add_fusion.sc, bf16[2048,256]{1,0:T(8,128)(2,1)} %pts.1, bf16[256,256]{1,0:T(8,128)(2,1)} %copy-done.3, bf16[256,256]{1,0:T(8,128)(2,1)} %copy-done.2, s32[27,2048]{1,0:T(8,128)} %bitcast.34, ...), custom_call_target="tpu_custom_call" | custom-call | flops 30000001024 | bytes 8000000 | tf_op jit(solution)/shard_map/conv/pallas_call | solution.py:112
  45.6 2.0 %collective-permute-start.4 = (bf16[1024,256]{1,0:T(8,128)(2,1)}, bf16[1024,256]{1,0:T(8,128)(2,1)}, u32[]{:S(2)}, u32[]{:S(2)}) collective-permute-start(bf16[1024,256]{1,0:T(8,128)(2,1)} %get-tuple-element.19), channel_id=1, source_target_pairs={{0,1},{1,0},{2,3},{3,2},{4,5},{5,4},{6,7},{7,6},{8,9},{9,8},{10,11... | collective-permute-start | bytes 1572872 | tf_op jit(solution)/shard_map/ppermute | solution.py:471
  47.7 0.1 collective-permute-start.7
  47.7 0.4 collective-permute-start.8
  48.2 0.1 collective-permute-start.11
  48.3 0.4 collective-permute-start.13
  48.7 1.1 collective-permute-done.8.qbo
  49.8 2.9 %collective-permute-start.5 = (bf16[512,256]{1,0:T(8,128)(2,1)}, bf16[512,256]{1,0:T(8,128)(2,1)}, u32[]{:S(2)}, u32[]{:S(2)}) collective-permute-start(bf16[512,256]{1,0:T(8,128)(2,1)} %get-tuple-element.20), channel_id=1, source_target_pairs={{0,2},{2,4},{4,6},{6,8},{8,10},{10,12},{12,14},{14,16},{16,18},{18... | collective-permute-start | bytes 786440 | tf_op jit(solution)/shard_map/ppermute | solution.py:496
  52.7 1.3 collective-permute-start.6
  54.0 23.9 %near.1 = (f32[4,2,256,256]{3,2,1,0:T(8,128)}, bf16[1024,256]{1,0:T(8,128)(2,1)}, f32[8,128]{1,0:T(8,128)}) custom-call(s32[3]{0:T(128)} %pad_add_fusion.sc, s32[1,256]{1,0:T(1,128)} %bitcast.42, bf16[32,32,256]{2,1,0:T(8,128)(2,1)} %bitcast.32, bf16[32,32,256]{2,1,0:T(8,128)(2,1)} %bitcast.12.oth, bf16[3,256,128]{2,1,0:T(8,128)(2,1)} %bitcast.36, ...), custom_call_target="tpu_custom_call" | custom-call | flops 20000000000 | bytes 8000000 | tf_op jit(solution)/shard_map/near/pallas_call | solution.py:112
  78.0 0.1 collective-permute-start.9
  78.1 0.5 collective-permute-start.10
  78.6 0.1 collective-permute-start.12
  78.7 1.6 collective-permute-done.12
  80.3 45.8 %far.1 = bf16[2048,256]{1,0:T(8,128)(2,1)} custom-call(s32[3]{0:T(128)} %pad_add_fusion.sc, s32[64]{0:T(128)} %slice_reduce_fusion.sel, s32[1,256]{1,0:T(1,128)} %bitcast.43, bf16[32,32,256]{2,1,0:T(8,128)(2,1)} %bitcast.33, bf16[32,32,256]{2,1,0:T(8,128)(2,1)} %bitcast.12.oth, bf16[16,32,256]{2,1,0:T(8,128)(2,1)} %bitcast.14.lo_own, ...), custom_call_target="tpu_custom_call" | custom-call | flops 20000000000 | bytes 8000000 | tf_op jit(solution)/shard_map/far/pallas_call | solution.py:112
  126.2 0.0 copy-start
  126.2 43.3 %all_to_all.17.own = bf16[64,32,256]{2,1,0:T(8,128)(2,1)S(1)} all-to-all(bf16[64,32,256]{2,1,0:T(8,128)(2,1)} %bitcast.29), channel_id=1, replica_groups=mesh['pts'=64,'grp'=2] {'pts'}, dimensions={0} | all-to-all | bytes 2097152 | tf_op jit(solution)/shard_map/all_to_all | solution.py:507
  169.5 1.8 collective-permute-start.14
  171.3 2.3 %collective-permute-done.14 = bf16[2048,256]{1,0:T(8,128)(2,1)S(1)} collective-permute-done((bf16[2048,256]{1,0:T(8,128)(2,1)S(1)}, bf16[2048,256]{1,0:T(8,128)(2,1)S(1)}, u32[]{:S(2)}, u32[]{:S(2)}) %collective-permute-start.14) | collective-permute-done | bytes 1048608 | tf_op jit(solution)/shard_map/ppermute | solution.py:471
  173.6 2.6 %relabel.1 = bf16[2048,256]{1,0:T(8,128)(2,1)} custom-call(s32[3]{0:T(128)S(1)} %copy-done.1, s32[2048]{0:T(1024)S(1)} %copy-done, s32[16,128]{1,0:T(8,128)S(1)} %bitcast.28, bf16[64,32,256]{2,1,0:T(8,128)(2,1)S(1)} %all_to_all.17.own, bf16[64,32,256]{2,1,0:T(8,128)(2,1)S(1)} %bitcast.27), custom_call_target="tpu_custom_call" | custom-call | tf_op jit(solution)/shard_map/relabel/pallas_call | solution.py:449
  (22 shorter events, 0.1 us)
Async XLA Ops:
  0.0 25.3 %collective-permute-start.2 = (bf16[6912,128]{1,0:T(8,128)(2,1)}, bf16[6912,128]{1,0:T(8,128)(2,1)}, u32[]{:S(2)}, u32[]{:S(2)}) collective-permute-start(bf16[6912,128]{1,0:T(8,128)(2,1)} %bitcast.30), channel_id=1, source_target_pairs={{0,1},{1,0},{2,3},{3,2},{4,5},{5,4},{6,7},{7,6},{8,9},{9,8},{10,11... | collective-permute-start | bytes 5308424 | tf_op jit(solution)/shard_map/ppermute | solution.py:471
  1.4 23.1 %collective-permute-start.3 = (f32[128]{0:T(128)}, f32[128]{0:T(128)S(1)}, u32[]{:S(2)}, u32[]{:S(2)}) collective-permute-start(f32[128]{0:T(128)} %param.24), channel_id=1, source_target_pairs={{0,1},{1,0},{2,3},{3,2},{4,5},{5,4},{6,7},{7,6},{8,9},{9,8},{10,11... | collective-permute-start | bytes 1544 | tf_op jit(solution)/shard_map/ppermute | solution.py:471
  3.1 19.6 %all-to-all-start = ((s32[64,1,128]{2,1,0:T(1,128)}), s32[64,1,128]{2,1,0:T(1,128)S(1)}, u32[]{:S(2)}, u32[]{:S(2)}) async-start(s32[64,1,128]{2,1,0:T(1,128)} %broadcast_in_dim.56), calls=%async_computation | async-start | bytes 65536 | tf_op jit(solution)/shard_map/all_to_all | solution.py:483
  15.3 9.2 %collective-permute-start.1 = (bf16[256,256]{1,0:T(8,128)(2,1)S(1)}, bf16[256,256]{1,0:T(8,128)(2,1)S(1)}, u32[]{:S(2)}, u32[]{:S(2)}) collective-permute-start(bf16[256,256]{1,0:T(8,128)(2,1)S(1)} %get-tuple-element.29), channel_id=1, source_target_pairs={{2,0},{4,2},{6,4},{8,6},{10,8},{12,10},{14,12},{16,14},{18,16},{20... | collective-permute-start | bytes 393224 | tf_op jit(solution)/shard_map/ppermute | solution.py:478
  16.6 7.9 %collective-permute-start = (bf16[256,256]{1,0:T(8,128)(2,1)S(1)}, bf16[256,256]{1,0:T(8,128)(2,1)S(1)}, u32[]{:S(2)}, u32[]{:S(2)}) collective-permute-start(bf16[256,256]{1,0:T(8,128)(2,1)S(1)} %get-tuple-element.30), channel_id=1, source_target_pairs={{0,2},{2,4},{4,6},{6,8},{8,10},{10,12},{12,14},{14,16},{16,18},{18... | collective-permute-start | bytes 393224 | tf_op jit(solution)/shard_map/ppermute | solution.py:477
  24.5 0.7 copy-start.3
  24.5 0.7 copy-start.4
  24.5 0.7 copy-start.2
  45.6 8.4 %collective-permute-start.4 = (bf16[1024,256]{1,0:T(8,128)(2,1)}, bf16[1024,256]{1,0:T(8,128)(2,1)}, u32[]{:S(2)}, u32[]{:S(2)}) collective-permute-start(bf16[1024,256]{1,0:T(8,128)(2,1)} %get-tuple-element.19), channel_id=1, source_target_pairs={{0,1},{1,0},{2,3},{3,2},{4,5},{5,4},{6,7},{7,6},{8,9},{9,8},{10,11... | collective-permute-start | bytes 1572872 | tf_op jit(solution)/shard_map/ppermute | solution.py:471
  47.7 5.1 %collective-permute-start.7 = (bf16[3,256,128]{2,1,0:T(8,128)(2,1)}, bf16[3,256,128]{2,1,0:T(8,128)(2,1)}, u32[]{:S(2)}, u32[]{:S(2)}) collective-permute-start(bf16[3,256,128]{2,1,0:T(8,128)(2,1)} %bitcast.35), channel_id=1, source_target_pairs={{0,1},{1,0},{2,3},{3,2},{4,5},{5,4},{6,7},{7,6},{8,9},{9,8},{10,11... | collective-permute-start | bytes 589832 | tf_op jit(solution)/shard_map/ppermute | solution.py:471
  47.7 2.1 %collective-permute-start.8 = (f32[3,128]{1,0:T(4,128)}, f32[3,128]{1,0:T(4,128)}, u32[]{:S(2)}, u32[]{:S(2)}) collective-permute-start(f32[3,128]{1,0:T(4,128)} %qbm.3), channel_id=1, source_target_pairs={{0,1},{1,0},{2,3},{3,2},{4,5},{5,4},{6,7},{7,6},{8,9},{9,8},{10,11... | collective-permute-start | bytes 4616 | tf_op jit(solution)/shard_map/ppermute | solution.py:471
  48.2 32.1 %collective-permute-start.11 = (bf16[256,512]{1,0:T(8,128)(2,1)}, bf16[256,512]{1,0:T(8,128)(2,1)}, u32[]{:S(2)}, u32[]{:S(2)}) collective-permute-start(bf16[256,512]{1,0:T(8,128)(2,1)} %f1m.1), channel_id=1, source_target_pairs={{0,1},{1,0},{2,3},{3,2},{4,5},{5,4},{6,7},{7,6},{8,9},{9,8},{10,11... | collective-permute-start | bytes 786440 | tf_op jit(solution)/shard_map/ppermute | solution.py:471
  48.3 32.1 %collective-permute-start.13 = (bf16[512,256]{1,0:T(8,128)(2,1)}, bf16[512,256]{1,0:T(8,128)(2,1)}, u32[]{:S(2)}, u32[]{:S(2)}) collective-permute-start(bf16[512,256]{1,0:T(8,128)(2,1)} %f2m.1), channel_id=1, source_target_pairs={{0,1},{1,0},{2,3},{3,2},{4,5},{5,4},{6,7},{7,6},{8,9},{9,8},{10,11... | collective-permute-start | bytes 786440 | tf_op jit(solution)/shard_map/ppermute | solution.py:471
  49.8 28.1 %collective-permute-start.5 = (bf16[512,256]{1,0:T(8,128)(2,1)}, bf16[512,256]{1,0:T(8,128)(2,1)}, u32[]{:S(2)}, u32[]{:S(2)}) collective-permute-start(bf16[512,256]{1,0:T(8,128)(2,1)} %get-tuple-element.20), channel_id=1, source_target_pairs={{0,2},{2,4},{4,6},{6,8},{8,10},{10,12},{12,14},{14,16},{16,18},{18... | collective-permute-start | bytes 786440 | tf_op jit(solution)/shard_map/ppermute | solution.py:496
  52.7 25.2 %collective-permute-start.6 = (bf16[512,256]{1,0:T(8,128)(2,1)}, bf16[512,256]{1,0:T(8,128)(2,1)}, u32[]{:S(2)}, u32[]{:S(2)}) collective-permute-start(bf16[512,256]{1,0:T(8,128)(2,1)} %get-tuple-element.21), channel_id=1, source_target_pairs={{2,0},{4,2},{6,4},{8,6},{10,8},{12,10},{14,12},{16,14},{18,16},{20... | collective-permute-start | bytes 786440 | tf_op jit(solution)/shard_map/ppermute | solution.py:497
  78.0 2.3 %collective-permute-start.9 = (bf16[512,256]{1,0:T(8,128)(2,1)}, bf16[512,256]{1,0:T(8,128)(2,1)}, u32[]{:S(2)}, u32[]{:S(2)}) collective-permute-start(bf16[512,256]{1,0:T(8,128)(2,1)} %collective-permute-done.5), channel_id=1, source_target_pairs={{0,1},{1,0},{2,3},{3,2},{4,5},{5,4},{6,7},{7,6},{8,9},{9,8},{10,11... | collective-permute-start | bytes 786440 | tf_op jit(solution)/shard_map/ppermute | solution.py:471
  78.1 2.3 %collective-permute-start.10 = (bf16[512,256]{1,0:T(8,128)(2,1)}, bf16[512,256]{1,0:T(8,128)(2,1)}, u32[]{:S(2)}, u32[]{:S(2)}) collective-permute-start(bf16[512,256]{1,0:T(8,128)(2,1)} %collective-permute-done.6), channel_id=1, source_target_pairs={{0,1},{1,0},{2,3},{3,2},{4,5},{5,4},{6,7},{7,6},{8,9},{9,8},{10,11... | collective-permute-start | bytes 786440 | tf_op jit(solution)/shard_map/ppermute | solution.py:471
  78.6 1.7 collective-permute-start.12
  126.2 47.4 %copy-start = (s32[2048]{0:T(1024)S(1)}, s32[2048]{0:T(1024)}, u32[]{:S(2)}) copy-start(s32[2048]{0:T(1024)} %zs.1) | copy-start | bytes 24580
  126.2 47.4 %copy-start.1 = (s32[3]{0:T(128)S(1)}, s32[3]{0:T(128)}, u32[]{:S(2)}) copy-start(s32[3]{0:T(128)} %pad_add_fusion.sc) | copy-start | bytes 40
  169.5 4.0 %collective-permute-start.14 = (bf16[2048,256]{1,0:T(8,128)(2,1)S(1)}, bf16[2048,256]{1,0:T(8,128)(2,1)S(1)}, u32[]{:S(2)}, u32[]{:S(2)}) collective-permute-start(bf16[2048,256]{1,0:T(8,128)(2,1)S(1)} %bitcast.26), channel_id=1, source_target_pairs={{0,1},{1,0},{2,3},{3,2},{4,5},{5,4},{6,7},{7,6},{8,9},{9,8},{10,11... | collective-permute-start | bytes 3145736 | tf_op jit(solution)/shard_map/ppermute | solution.py:471
where the time goes:
time: 176 us
  Pallas kernels  92.7 us (53%)
  blocking collectives  43.3 us (25%)
  starting transfers between devices  27.6 us (16%)
  waiting for transfers between devices  6.55 us (4%)
  local copies, waits for them, and re-layouts  5.13 us (3%)
    pallas_call x3, Pallas kernels, call(): pl.pallas_call(kernel, out_shape=out_shape, in_specs=[pl.BlockSpec(memory...  90.1 us
    all_to_all x1, blocking collectives, local(): got = lax.all_to_all(send, 'pts', split_axis=0, concat_axis=0, tiled=True)  43.3 us
    all_to_all x1, starting transfers between devices, local(): lax.all_to_all(wanted, 'pts', split_axis=0, concat_axis=0, tiled=True)  11.2 us
    ppermute x11, starting transfers between devices, swap(): return lax.ppermute(x, 'grp', [(0, 1), (1, 0)])  6.9 us
    ppermute x11, waiting for transfers between devices, swap(): return lax.ppermute(x, 'grp', [(0, 1), (1, 0)])  5.1 us
    ppermute x1, starting transfers between devices, local(): low = lax.ppermute(points[rows - 256:], 'pts', forward)  3.99 us
  transfers between devices with their start and end apart: 16, of which 4 were waited for; matrix products, arithmetic and copies ran while one was open for 3% of the time, Pallas kernels for 14%

commit v1 on v0

--- a/solution.py
+++ b/solution.py
@@ -408,7 +408,7 @@
 
     def place(d, _):
         send[pl.ds(pl.multiple_of(32 * d, 32), 32), :] = OUT[
-            pl.ds(pl.multiple_of(32 * sel[d], 32), 32), :
+            pl.ds(pl.multiple_of(32 * sel[d, 0, 0], 32), 32), :
         ]
         return 0
 
@@ -476,14 +476,15 @@
     order = zorder.reshape(16, 128)
     low = lax.ppermute(points[rows - 256 :], "pts", forward)
     high = lax.ppermute(points[:256], "pts", backward)
+    conv_m = conv_w.reshape(27 * 256, 128)
+    conv_o, bias_o = swap(conv_m), swap(conv_b)
     sources = jnp.arange(peers, dtype=jnp.int32)[:, None]
     run = zorder[::64][None, :]
     wanted = jnp.max(jnp.where(run // rows == sources, run % rows // 64, 0), axis=1)
     wanted = jnp.broadcast_to(wanted[:, None, None], (peers, 1, 128))
-    sel = lax.all_to_all(wanted, "pts", split_axis=0, concat_axis=0, tiled=True)[:, 0, 0]
+    wanted, bias_o = lax.optimization_barrier((wanted, bias_o))
+    sel = lax.all_to_all(wanted, "pts", split_axis=0, concat_axis=0, tiled=True)
     sel, low = lax.optimization_barrier((sel, low))
-    conv_m = conv_w.reshape(27 * 256, 128)
-    conv_o, bias_o = swap(conv_m), swap(conv_b)
     scalars = jnp.stack([g, me * rows, jnp.int32(rows * peers)])
     section_one, normed, lo_half, hi_half = conv_call(
         scalars, points, low, high, neighbours.T, conv_m, conv_o, conv_b[None], bias_o[None],
@@ -492,7 +493,7 @@
     qkv_m = jnp.transpose(qkv_w, (1, 0, 2))
     weights = (qkv_m, swap(qkv_m), qkv_b, swap(qkv_b))
     fc1_o, fc2_o, b1_o = swap(fc1_w), swap(fc2_w), swap(fc1_b)
-    other = swap(normed)
+    other, b1_o = lax.optimization_barrier((swap(normed), b1_o))
     lo_own = lax.ppermute(lo_half, "pts", forward)
     hi_own = lax.ppermute(hi_half, "pts", backward)
     acc, query, most = near_call(scalars, patch_len[None], pieces(normed), pieces(other), *weights)

time: 176 us -> 180 us (1.023); the launches traced: 176 us -> 182 us
  blocking collectives: 43.3 us -> 36.7 us
  waiting for transfers between devices: 6.55 us -> 13 us
  starting transfers between devices: 27.6 us -> 32.1 us
  Pallas kernels: 92.7 us -> 95.2 us
    all_to_all x1, blocking collectives: 43.3 us -> 36.7 us  [local(): got = lax.all_to_all(send, 'pts', split_axis=0, concat_axis=0, tiled=True)]
    all_to_all x1, waiting for transfers between devices: 1.45 us -> 7.72 us  [local(): sel = lax.all_to_all(wanted, 'pts', split_axis=0, concat_axis=0, tiled=True)]
    all_to_all x1, starting transfers between devices: 11.2 us -> 14.8 us  [local(): sel = lax.all_to_all(wanted, 'pts', split_axis=0, concat_axis=0, tiled=True)]
    pallas_call x3, Pallas kernels: 90.1 us -> 92.6 us  [call(): pl.pallas_call(kernel, out_shape=out_shape, in_specs=[pl.BlockSpec(memory...]
    slice x1 -> x0, local copies, waits for them, and re-layouts: 1.86 us -> none  [local(): lax.all_to_all(wanted, 'pts', split_axis=0, concat_axis=0, tiled=True)]
  transfers between devices with their start and end apart: 16 -> 16, of which waited for: 4 -> 5; matrix products, arithmetic and copies ran while one was open for 3% -> 2% of each run, Pallas kernels for 14% -> 14%
where the time goes in v1:
time: 180 us; the launch traced here: 182 us
  Pallas kernels  95.2 us (53%)
  blocking collectives  36.7 us (20%)
  starting transfers between devices  32.1 us (18%)
  waiting for transfers between devices  13 us (7%)
  local copies, waits for them, and re-layouts  4.43 us (2%)
    pallas_call x3, Pallas kernels, call(): pl.pallas_call(kernel, out_shape=out_shape, in_specs=[pl.BlockSpec(memory...  92.6 us
    all_to_all x1, blocking collectives, local(): got = lax.all_to_all(send, 'pts', split_axis=0, concat_axis=0, tiled=True)  36.7 us
    all_to_all x1, starting transfers between devices, local(): sel = lax.all_to_all(wanted, 'pts', split_axis=0, concat_axis=0, tiled=True)  14.8 us
    ppermute x11, starting transfers between devices, swap(): return lax.ppermute(x, 'grp', [(0, 1), (1, 0)])  7.77 us
    all_to_all x1, waiting for transfers between devices, local(): sel = lax.all_to_all(wanted, 'pts', split_axis=0, concat_axis=0, tiled=True)  7.72 us
    ppermute x11, waiting for transfers between devices, swap(): return lax.ppermute(x, 'grp', [(0, 1), (1, 0)])  5.22 us
    ppermute x1, starting transfers between devices, local(): low = lax.ppermute(points[rows - 256:], 'pts', forward)  3.99 us
  transfers between devices with their start and end apart: 16, of which 5 were waited for; matrix products, arithmetic and copies ran while one was open for 2% of the time, Pallas kernels for 14%

profile of v1, /device:TPU:1, one launch (start us, length us, event | category | flops | bytes accessed | tf_op | source)
XLA Modules:
  0.0 182.2 jit_solution(10107567364001693152)
XLA Ops:
  0.0 1.4 collective-permute-start.3
  1.4 1.0 fusion
  2.4 1.3 collective-permute-start.2
  3.7 4.0 %collective-permute-start.1 = (bf16[256,256]{1,0:T(8,128)(2,1)S(1)}, bf16[256,256]{1,0:T(8,128)(2,1)S(1)}, u32[]{:S(2)}, u32[]{:S(2)}) collective-permute-start(bf16[256,256]{1,0:T(8,128)(2,1)S(1)} %get-tuple-element.38), channel_id=1, source_target_pairs={{0,2},{2,4},{4,6},{6,8},{8,10},{10,12},{12,14},{14,16},{16,18},{18... | collective-permute-start | bytes 393224 | tf_op jit(solution)/shard_map/ppermute | solution.py:477
  7.7 0.8 slice.9
  8.5 0.1 select_reduce_fusion
  8.7 0.7 broadcast_in_dim.56
  9.4 14.8 %all-to-all-start = ((s32[64,1,128]{2,1,0:T(1,128)}), s32[64,1,128]{2,1,0:T(1,128)S(1)}, u32[]{:S(2)}, u32[]{:S(2)}) async-start(s32[64,1,128]{2,1,0:T(1,128)} %broadcast_in_dim.56), calls=%async_computation | async-start | bytes 65536 | tf_op jit(solution)/shard_map/all_to_all | solution.py:486
  24.2 0.6 pad_add_fusion.sc
  24.9 7.7 %all-to-all-done.sel = s32[64,1,128]{2,1,0:T(1,128)S(1)} async-done(((s32[64,1,128]{2,1,0:T(1,128)}), s32[64,1,128]{2,1,0:T(1,128)S(1)}, u32[]{:S(2)}, u32[]{:S(2)}) %all-to-all-start) | async-done | bytes 32800 | tf_op jit(solution)/shard_map/all_to_all | solution.py:486
  32.6 0.6 copy-done.2
  33.2 1.3 copy-done.3
  34.5 20.3 %conv.1 = (bf16[1024,256]{1,0:T(8,128)(2,1)}, bf16[1024,256]{1,0:T(8,128)(2,1)}, bf16[512,256]{1,0:T(8,128)(2,1)}, bf16[512,256]{1,0:T(8,128)(2,1)}) custom-call(s32[3]{0:T(128)} %pad_add_fusion.sc, bf16[2048,256]{1,0:T(8,128)(2,1)} %pts.1, bf16[256,256]{1,0:T(8,128)(2,1)} %copy-done.5, bf16[256,256]{1,0:T(8,128)(2,1)} %copy-done.4, s32[27,2048]{1,0:T(8,128)} %bitcast.34, ...), custom_call_target="tpu_custom_call" | custom-call | flops 30000001024 | bytes 8000000 | tf_op jit(solution)/shard_map/conv/pallas_call | solution.py:112
  54.8 2.6 %collective-permute-start.4 = (bf16[1024,256]{1,0:T(8,128)(2,1)}, bf16[1024,256]{1,0:T(8,128)(2,1)}, u32[]{:S(2)}, u32[]{:S(2)}) collective-permute-start(bf16[1024,256]{1,0:T(8,128)(2,1)} %get-tuple-element.25), channel_id=1, source_target_pairs={{0,1},{1,0},{2,3},{3,2},{4,5},{5,4},{6,7},{7,6},{8,9},{9,8},{10,11... | collective-permute-start | bytes 1572872 | tf_op jit(solution)/shard_map/ppermute | solution.py:471
  57.4 0.1 collective-permute-start.8
  57.5 0.4 collective-permute-start.5
  57.9 0.1 collective-permute-start.9
  58.0 0.4 collective-permute-start.12
  58.4 1.1 collective-permute-done.5
  59.5 0.4 collective-permute-start.13
  59.9 2.9 %collective-permute-start.6 = (bf16[512,256]{1,0:T(8,128)(2,1)}, bf16[512,256]{1,0:T(8,128)(2,1)}, u32[]{:S(2)}, u32[]{:S(2)}) collective-permute-start(bf16[512,256]{1,0:T(8,128)(2,1)} %get-tuple-element.27), channel_id=1, source_target_pairs={{0,2},{2,4},{4,6},{6,8},{8,10},{10,12},{12,14},{14,16},{16,18},{18... | collective-permute-start | bytes 786440 | tf_op jit(solution)/shard_map/ppermute | solution.py:497
  62.8 1.3 collective-permute-start.7
  64.1 24.7 %near.1 = (f32[4,2,256,256]{3,2,1,0:T(8,128)}, bf16[1024,256]{1,0:T(8,128)(2,1)}, f32[8,128]{1,0:T(8,128)}) custom-call(s32[3]{0:T(128)} %pad_add_fusion.sc, s32[1,256]{1,0:T(1,128)} %bitcast.42, bf16[32,32,256]{2,1,0:T(8,128)(2,1)} %bitcast.32, bf16[32,32,256]{2,1,0:T(8,128)(2,1)} %bitcast.12.oth, bf16[3,256,128]{2,1,0:T(8,128)(2,1)} %bitcast.36, ...), custom_call_target="tpu_custom_call" | custom-call | flops 20000000000 | bytes 8000000 | tf_op jit(solution)/shard_map/near/pallas_call | solution.py:112
  88.9 0.5 collective-permute-start.10
  89.4 0.1 collective-permute-start.11
  89.5 1.4 collective-permute-done.10
  90.9 0.4 collective-permute-done.11
  91.3 47.6 %far.1 = bf16[2048,256]{1,0:T(8,128)(2,1)} custom-call(s32[3]{0:T(128)} %pad_add_fusion.sc, s32[64,1,128]{2,1,0:T(1,128)} %copy-done.2, s32[1,256]{1,0:T(1,128)} %bitcast.43, bf16[32,32,256]{2,1,0:T(8,128)(2,1)} %bitcast.33, bf16[32,32,256]{2,1,0:T(8,128)(2,1)} %bitcast.12.oth, bf16[16,32,256]{2,1,0:T(8,128)(2,1)} %bitcast.14.lo_own, ...), custom_call_target="tpu_custom_call" | custom-call | flops 20000000000 | bytes 8000000 | tf_op jit(solution)/shard_map/far/pallas_call | solution.py:112
  138.9 36.7 %all_to_all.17.own = bf16[64,32,256]{2,1,0:T(8,128)(2,1)S(1)} all-to-all(bf16[64,32,256]{2,1,0:T(8,128)(2,1)} %bitcast.29), channel_id=1, replica_groups=mesh['pts'=64,'grp'=2] {'pts'}, dimensions={0} | all-to-all | bytes 2097152 | tf_op jit(solution)/shard_map/all_to_all | solution.py:508
  175.6 1.8 collective-permute-start.14
  177.4 2.3 %collective-permute-done.14 = bf16[2048,256]{1,0:T(8,128)(2,1)S(1)} collective-permute-done((bf16[2048,256]{1,0:T(8,128)(2,1)S(1)}, bf16[2048,256]{1,0:T(8,128)(2,1)S(1)}, u32[]{:S(2)}, u32[]{:S(2)}) %collective-permute-start.14) | collective-permute-done | bytes 1048608 | tf_op jit(solution)/shard_map/ppermute | solution.py:471
  179.6 2.6 %relabel.1 = bf16[2048,256]{1,0:T(8,128)(2,1)} custom-call(s32[3]{0:T(128)S(1)} %copy-done.1, s32[2048]{0:T(1024)S(1)} %copy-done, s32[16,128]{1,0:T(8,128)S(1)} %bitcast.28, bf16[64,32,256]{2,1,0:T(8,128)(2,1)S(1)} %all_to_all.17.own, bf16[64,32,256]{2,1,0:T(8,128)(2,1)S(1)} %bitcast.27), custom_call_target="tpu_custom_call" | custom-call | tf_op jit(solution)/shard_map/relabel/pallas_call | solution.py:449
  (25 shorter events, 0.1 us)
Async XLA Ops:
  0.0 33.2 %collective-permute-start.3 = (bf16[6912,128]{1,0:T(8,128)(2,1)}, bf16[6912,128]{1,0:T(8,128)(2,1)S(1)}, u32[]{:S(2)}, u32[]{:S(2)}) collective-permute-start(bf16[6912,128]{1,0:T(8,128)(2,1)} %bitcast.30), channel_id=1, source_target_pairs={{0,1},{1,0},{2,3},{3,2},{4,5},{5,4},{6,7},{7,6},{8,9},{9,8},{10,11... | collective-permute-start | bytes 5308424 | tf_op jit(solution)/shard_map/ppermute | solution.py:471
  1.4 7.2 %collective-permute-start = (f32[128]{0:T(128)}, f32[128]{0:T(128)S(1)}, u32[]{:S(2)}, u32[]{:S(2)}) collective-permute-start(f32[128]{0:T(128)} %param.24), channel_id=1, source_target_pairs={{0,1},{1,0},{2,3},{3,2},{4,5},{5,4},{6,7},{7,6},{8,9},{9,8},{10,11... | collective-permute-start | bytes 1544 | tf_op jit(solution)/shard_map/ppermute | solution.py:471
  2.4 30.2 %collective-permute-start.2 = (bf16[256,256]{1,0:T(8,128)(2,1)S(1)}, bf16[256,256]{1,0:T(8,128)(2,1)S(1)}, u32[]{:S(2)}, u32[]{:S(2)}) collective-permute-start(bf16[256,256]{1,0:T(8,128)(2,1)S(1)} %get-tuple-element.37), channel_id=1, source_target_pairs={{2,0},{4,2},{6,4},{8,6},{10,8},{12,10},{14,12},{16,14},{18,16},{20... | collective-permute-start | bytes 393224 | tf_op jit(solution)/shard_map/ppermute | solution.py:478
  3.7 28.9 %collective-permute-start.1 = (bf16[256,256]{1,0:T(8,128)(2,1)S(1)}, bf16[256,256]{1,0:T(8,128)(2,1)S(1)}, u32[]{:S(2)}, u32[]{:S(2)}) collective-permute-start(bf16[256,256]{1,0:T(8,128)(2,1)S(1)} %get-tuple-element.38), channel_id=1, source_target_pairs={{0,2},{2,4},{4,6},{6,8},{8,10},{10,12},{12,14},{14,16},{16,18},{18... | collective-permute-start | bytes 393224 | tf_op jit(solution)/shard_map/ppermute | solution.py:477
  8.7 25.8 %copy-start.6 = (f32[128]{0:T(128)}, f32[128]{0:T(128)S(1)}, u32[]{:S(2)}) copy-start(f32[128]{0:T(128)S(1)} %collective-permute-done) | copy-start | bytes 1540
  9.4 23.2 %all-to-all-start = ((s32[64,1,128]{2,1,0:T(1,128)}), s32[64,1,128]{2,1,0:T(1,128)S(1)}, u32[]{:S(2)}, u32[]{:S(2)}) async-start(s32[64,1,128]{2,1,0:T(1,128)} %broadcast_in_dim.56), calls=%async_computation | async-start | bytes 65536 | tf_op jit(solution)/shard_map/all_to_all | solution.py:486
  32.6 0.6 copy-start.2
  32.6 1.9 %copy-start.5 = (bf16[256,256]{1,0:T(8,128)(2,1)}, bf16[256,256]{1,0:T(8,128)(2,1)S(1)}, u32[]{:S(2)}) copy-start(bf16[256,256]{1,0:T(8,128)(2,1)S(1)} %collective-permute-done.1.low) | copy-start | bytes 393220
  33.2 1.3 copy-start.4
  33.2 1.3 copy-start.3
  54.8 5.1 %collective-permute-start.4 = (bf16[1024,256]{1,0:T(8,128)(2,1)}, bf16[1024,256]{1,0:T(8,128)(2,1)}, u32[]{:S(2)}, u32[]{:S(2)}) collective-permute-start(bf16[1024,256]{1,0:T(8,128)(2,1)} %get-tuple-element.25), channel_id=1, source_target_pairs={{0,1},{1,0},{2,3},{3,2},{4,5},{5,4},{6,7},{7,6},{8,9},{9,8},{10,11... | collective-permute-start | bytes 1572872 | tf_op jit(solution)/shard_map/ppermute | solution.py:471
  57.4 6.7 %collective-permute-start.8 = (bf16[3,256,128]{2,1,0:T(8,128)(2,1)}, bf16[3,256,128]{2,1,0:T(8,128)(2,1)}, u32[]{:S(2)}, u32[]{:S(2)}) collective-permute-start(bf16[3,256,128]{2,1,0:T(8,128)(2,1)} %bitcast.35), channel_id=1, source_target_pairs={{0,1},{1,0},{2,3},{3,2},{4,5},{5,4},{6,7},{7,6},{8,9},{9,8},{10,11... | collective-permute-start | bytes 589832 | tf_op jit(solution)/shard_map/ppermute | solution.py:471
  57.5 2.1 %collective-permute-start.5 = (f32[512]{0:T(512)}, f32[512]{0:T(512)}, u32[]{:S(2)}, u32[]{:S(2)}) collective-permute-start(f32[512]{0:T(512)} %param.35), channel_id=1, source_target_pairs={{0,1},{1,0},{2,3},{3,2},{4,5},{5,4},{6,7},{7,6},{8,9},{9,8},{10,11... | collective-permute-start | bytes 6152 | tf_op jit(solution)/shard_map/ppermute | solution.py:471
  57.9 4.9 %collective-permute-start.9 = (f32[3,128]{1,0:T(4,128)}, f32[3,128]{1,0:T(4,128)}, u32[]{:S(2)}, u32[]{:S(2)}) collective-permute-start(f32[3,128]{1,0:T(4,128)} %qbm.3), channel_id=1, source_target_pairs={{0,1},{1,0},{2,3},{3,2},{4,5},{5,4},{6,7},{7,6},{8,9},{9,8},{10,11... | collective-permute-start | bytes 4616 | tf_op jit(solution)/shard_map/ppermute | solution.py:471
  58.0 31.5 %collective-permute-start.12 = (bf16[256,512]{1,0:T(8,128)(2,1)}, bf16[256,512]{1,0:T(8,128)(2,1)}, u32[]{:S(2)}, u32[]{:S(2)}) collective-permute-start(bf16[256,512]{1,0:T(8,128)(2,1)} %f1m.1), channel_id=1, source_target_pairs={{0,1},{1,0},{2,3},{3,2},{4,5},{5,4},{6,7},{7,6},{8,9},{9,8},{10,11... | collective-permute-start | bytes 786440 | tf_op jit(solution)/shard_map/ppermute | solution.py:471
  59.5 30.0 %collective-permute-start.13 = (bf16[512,256]{1,0:T(8,128)(2,1)}, bf16[512,256]{1,0:T(8,128)(2,1)}, u32[]{:S(2)}, u32[]{:S(2)}) collective-permute-start(bf16[512,256]{1,0:T(8,128)(2,1)} %f2m.1), channel_id=1, source_target_pairs={{0,1},{1,0},{2,3},{3,2},{4,5},{5,4},{6,7},{7,6},{8,9},{9,8},{10,11... | collective-permute-start | bytes 786440 | tf_op jit(solution)/shard_map/ppermute | solution.py:471
  59.9 28.9 %collective-permute-start.6 = (bf16[512,256]{1,0:T(8,128)(2,1)}, bf16[512,256]{1,0:T(8,128)(2,1)}, u32[]{:S(2)}, u32[]{:S(2)}) collective-permute-start(bf16[512,256]{1,0:T(8,128)(2,1)} %get-tuple-element.27), channel_id=1, source_target_pairs={{0,2},{2,4},{4,6},{6,8},{8,10},{10,12},{12,14},{14,16},{16,18},{18... | collective-permute-start | bytes 786440 | tf_op jit(solution)/shard_map/ppermute | solution.py:497
  62.8 26.1 %collective-permute-start.7 = (bf16[512,256]{1,0:T(8,128)(2,1)}, bf16[512,256]{1,0:T(8,128)(2,1)}, u32[]{:S(2)}, u32[]{:S(2)}) collective-permute-start(bf16[512,256]{1,0:T(8,128)(2,1)} %get-tuple-element.28), channel_id=1, source_target_pairs={{2,0},{4,2},{6,4},{8,6},{10,8},{12,10},{14,12},{16,14},{18,16},{20... | collective-permute-start | bytes 786440 | tf_op jit(solution)/shard_map/ppermute | solution.py:498
  88.9 2.0 %collective-permute-start.10 = (bf16[512,256]{1,0:T(8,128)(2,1)}, bf16[512,256]{1,0:T(8,128)(2,1)}, u32[]{:S(2)}, u32[]{:S(2)}) collective-permute-start(bf16[512,256]{1,0:T(8,128)(2,1)} %collective-permute-done.6), channel_id=1, source_target_pairs={{0,1},{1,0},{2,3},{3,2},{4,5},{5,4},{6,7},{7,6},{8,9},{9,8},{10,11... | collective-permute-start | bytes 786440 | tf_op jit(solution)/shard_map/ppermute | solution.py:471
  89.4 1.9 %collective-permute-start.11 = (bf16[512,256]{1,0:T(8,128)(2,1)}, bf16[512,256]{1,0:T(8,128)(2,1)}, u32[]{:S(2)}, u32[]{:S(2)}) collective-permute-start(bf16[512,256]{1,0:T(8,128)(2,1)} %collective-permute-done.7), channel_id=1, source_target_pairs={{0,1},{1,0},{2,3},{3,2},{4,5},{5,4},{6,7},{7,6},{8,9},{9,8},{10,11... | collective-permute-start | bytes 786440 | tf_op jit(solution)/shard_map/ppermute | solution.py:471
  138.8 40.8 %copy-start = (s32[2048]{0:T(1024)S(1)}, s32[2048]{0:T(1024)}, u32[]{:S(2)}) copy-start(s32[2048]{0:T(1024)} %zs.1) | copy-start | bytes 24580
  138.8 40.8 %copy-start.1 = (s32[3]{0:T(128)S(1)}, s32[3]{0:T(128)}, u32[]{:S(2)}) copy-start(s32[3]{0:T(128)} %pad_add_fusion.sc) | copy-start | bytes 40
  175.6 4.1 %collective-permute-start.14 = (bf16[2048,256]{1,0:T(8,128)(2,1)S(1)}, bf16[2048,256]{1,0:T(8,128)(2,1)S(1)}, u32[]{:S(2)}, u32[]{:S(2)}) collective-permute-start(bf16[2048,256]{1,0:T(8,128)(2,1)S(1)} %bitcast.26), channel_id=1, source_target_pairs={{0,1},{1,0},{2,3},{3,2},{4,5},{5,4},{6,7},{7,6},{8,9},{9,8},{10,11... | collective-permute-start | bytes 3145736 | tf_op jit(solution)/shard_map/ppermute | solution.py:471

commit v2 on v1

--- a/solution.py
+++ b/solution.py
@@ -484,12 +484,12 @@
     wanted = jnp.broadcast_to(wanted[:, None, None], (peers, 1, 128))
     wanted, bias_o = lax.optimization_barrier((wanted, bias_o))
     sel = lax.all_to_all(wanted, "pts", split_axis=0, concat_axis=0, tiled=True)
-    sel, low = lax.optimization_barrier((sel, low))
     scalars = jnp.stack([g, me * rows, jnp.int32(rows * peers)])
     section_one, normed, lo_half, hi_half = conv_call(
         scalars, points, low, high, neighbours.T, conv_m, conv_o, conv_b[None], bias_o[None],
         cpe_w, cpe_b[None], cpe_gain[None], norm1_gain[None],
     )
+    sel, normed, lo_half, hi_half = lax.optimization_barrier((sel, normed, lo_half, hi_half))
     qkv_m = jnp.transpose(qkv_w, (1, 0, 2))
     weights = (qkv_m, swap(qkv_m), qkv_b, swap(qkv_b))
     fc1_o, fc2_o, b1_o = swap(fc1_w), swap(fc2_w), swap(fc1_b)

time: 180 us -> 176 us (0.978)
  blocking collectives: 36.7 us -> 44.8 us
  waiting for transfers between devices: 13 us -> 5.24 us
  Pallas kernels: 95.2 us -> 91.1 us
    all_to_all x1, blocking collectives: 36.7 us -> 44.8 us  [local(): got = lax.all_to_all(send, 'pts', split_axis=0, concat_axis=0, tiled=True)]
    all_to_all x1, waiting for transfers between devices: 7.72 us -> 0.01 us  [local(): sel = lax.all_to_all(wanted, 'pts', split_axis=0, concat_axis=0, tiled=True)]
    pallas_call x3, Pallas kernels: 92.6 us -> 88.5 us  [call(): pl.pallas_call(kernel, out_shape=out_shape, in_specs=[pl.BlockSpec(memory...]
  transfers between devices with their start and end apart: 16 -> 16, of which waited for: 5 -> 4; matrix products, arithmetic and copies ran while one was open for 2% -> 2% of each run, Pallas kernels for 14% -> 24%
where the time goes in v2:
time: 176 us; the launch traced here: 178 us
  Pallas kernels  91.1 us (52%)
  blocking collectives  44.8 us (25%)
  starting transfers between devices  32.1 us (18%)
  waiting for transfers between devices  5.24 us (3%)
  local copies, waits for them, and re-layouts  3.82 us (2%)
    pallas_call x3, Pallas kernels, call(): pl.pallas_call(kernel, out_shape=out_shape, in_specs=[pl.BlockSpec(memory...  88.5 us
    all_to_all x1, blocking collectives, local(): got = lax.all_to_all(send, 'pts', split_axis=0, concat_axis=0, tiled=True)  44.8 us
    all_to_all x1, starting transfers between devices, local(): sel = lax.all_to_all(wanted, 'pts', split_axis=0, concat_axis=0, tiled=True)  15.1 us
    ppermute x11, starting transfers between devices, swap(): return lax.ppermute(x, 'grp', [(0, 1), (1, 0)])  6.61 us
    ppermute x11, waiting for transfers between devices, swap(): return lax.ppermute(x, 'grp', [(0, 1), (1, 0)])  5.22 us
    ppermute x1, starting transfers between devices, local(): low = lax.ppermute(points[rows - 256:], 'pts', forward)  3.99 us
    ppermute x1, starting transfers between devices, local(): lo_own = lax.ppermute(lo_half, 'pts', forward)  3.84 us
  transfers between devices with their start and end apart: 16, of which 4 were waited for; matrix products, arithmetic and copies ran while one was open for 2% of the time, Pallas kernels for 24%

profile of v2, /device:TPU:1, one launch (start us, length us, event | category | flops | bytes accessed | tf_op | source)
XLA Modules:
  0.0 177.9 jit_solution(9818183582901608653)
XLA Ops:
  0.0 1.4 collective-permute-start.3
  1.4 1.0 fusion
  2.4 1.3 collective-permute-start.2
  3.7 4.0 %collective-permute-start.1 = (bf16[256,256]{1,0:T(8,128)(2,1)S(1)}, bf16[256,256]{1,0:T(8,128)(2,1)S(1)}, u32[]{:S(2)}, u32[]{:S(2)}) collective-permute-start(bf16[256,256]{1,0:T(8,128)(2,1)S(1)} %get-tuple-element.42), channel_id=1, source_target_pairs={{0,2},{2,4},{4,6},{6,8},{8,10},{10,12},{12,14},{14,16},{16,18},{18... | collective-permute-start | bytes 393224 | tf_op jit(solution)/shard_map/ppermute | solution.py:477
  7.7 0.8 slice.9
  8.5 0.1 select_reduce_fusion
  8.6 0.6 pad_add_fusion.sc
  9.2 0.7 broadcast_in_dim.56
  10.0 15.1 %all-to-all-start = ((s32[64,1,128]{2,1,0:T(1,128)}), s32[64,1,128]{2,1,0:T(1,128)}, u32[]{:S(2)}, u32[]{:S(2)}) async-start(s32[64,1,128]{2,1,0:T(1,128)} %broadcast_in_dim.56), calls=%async_computation | async-start | bytes 65536 | tf_op jit(solution)/shard_map/all_to_all | solution.py:486
  25.1 0.6 copy-done.2
  25.7 0.6 copy-done.3
  26.4 20.3 %conv.1 = (bf16[1024,256]{1,0:T(8,128)(2,1)}, bf16[1024,256]{1,0:T(8,128)(2,1)}, bf16[512,256]{1,0:T(8,128)(2,1)}, bf16[512,256]{1,0:T(8,128)(2,1)}) custom-call(s32[3]{0:T(128)} %pad_add_fusion.sc, bf16[2048,256]{1,0:T(8,128)(2,1)} %pts.1, bf16[256,256]{1,0:T(8,128)(2,1)} %copy-done.3, bf16[256,256]{1,0:T(8,128)(2,1)} %copy-done.2, s32[27,2048]{1,0:T(8,128)} %bitcast.34, ...), custom_call_target="tpu_custom_call" | custom-call | flops 30000001024 | bytes 8000000 | tf_op jit(solution)/shard_map/conv/pallas_call | solution.py:112
  46.7 1.4 collective-permute-start.4
  48.1 0.1 collective-permute-start.8
  48.2 0.4 collective-permute-start.5
  48.6 0.1 collective-permute-start.9
  48.7 0.4 collective-permute-start.12
  49.2 1.1 collective-permute-done.5
  50.3 0.4 collective-permute-start.13
  50.7 3.8 %collective-permute-start.6 = (bf16[512,256]{1,0:T(8,128)(2,1)}, bf16[512,256]{1,0:T(8,128)(2,1)}, u32[]{:S(2)}, u32[]{:S(2)}) collective-permute-start(bf16[512,256]{1,0:T(8,128)(2,1)} %get-tuple-element.31), channel_id=1, source_target_pairs={{0,2},{2,4},{4,6},{6,8},{8,10},{10,12},{12,14},{14,16},{16,18},{18... | collective-permute-start | bytes 786440 | tf_op jit(solution)/shard_map/ppermute | solution.py:497
  54.5 1.3 collective-permute-start.7
  55.8 23.1 %near.1 = (f32[4,2,256,256]{3,2,1,0:T(8,128)}, bf16[1024,256]{1,0:T(8,128)(2,1)}, f32[8,128]{1,0:T(8,128)}) custom-call(s32[3]{0:T(128)} %pad_add_fusion.sc, s32[1,256]{1,0:T(1,128)} %bitcast.42, bf16[32,32,256]{2,1,0:T(8,128)(2,1)} %bitcast.32, bf16[32,32,256]{2,1,0:T(8,128)(2,1)} %bitcast.12.oth, bf16[3,256,128]{2,1,0:T(8,128)(2,1)} %bitcast.36, ...), custom_call_target="tpu_custom_call" | custom-call | flops 20000000000 | bytes 8000000 | tf_op jit(solution)/shard_map/near/pallas_call | solution.py:112
  79.0 0.5 collective-permute-start.10
  79.5 0.1 collective-permute-start.11
  79.6 1.4 collective-permute-done.10
  81.0 0.4 collective-permute-done.11
  81.3 45.1 %far.1 = bf16[2048,256]{1,0:T(8,128)(2,1)} custom-call(s32[3]{0:T(128)} %pad_add_fusion.sc, s32[64,1,128]{2,1,0:T(1,128)} %all-to-all-done.sel, s32[1,256]{1,0:T(1,128)} %bitcast.43, bf16[32,32,256]{2,1,0:T(8,128)(2,1)} %bitcast.33, bf16[32,32,256]{2,1,0:T(8,128)(2,1)} %bitcast.12.oth, bf16[16,32,256]{2,1,0:T(8,128)(2,1)} %bitcast.14.lo_own, ...), custom_call_target="tpu_custom_call" | custom-call | flops 20000000000 | bytes 8000000 | tf_op jit(solution)/shard_map/far/pallas_call | solution.py:112
  126.5 0.0 copy-start
  126.5 44.8 %all_to_all.17.own = bf16[64,32,256]{2,1,0:T(8,128)(2,1)S(1)} all-to-all(bf16[64,32,256]{2,1,0:T(8,128)(2,1)} %bitcast.29), channel_id=1, replica_groups=mesh['pts'=64,'grp'=2] {'pts'}, dimensions={0} | all-to-all | bytes 2097152 | tf_op jit(solution)/shard_map/all_to_all | solution.py:508
  171.3 1.8 collective-permute-start.14
  173.0 2.3 %collective-permute-done.14 = bf16[2048,256]{1,0:T(8,128)(2,1)S(1)} collective-permute-done((bf16[2048,256]{1,0:T(8,128)(2,1)S(1)}, bf16[2048,256]{1,0:T(8,128)(2,1)S(1)}, u32[]{:S(2)}, u32[]{:S(2)}) %collective-permute-start.14) | collective-permute-done | bytes 1048608 | tf_op jit(solution)/shard_map/ppermute | solution.py:471
  175.3 2.6 %relabel.1 = bf16[2048,256]{1,0:T(8,128)(2,1)} custom-call(s32[3]{0:T(128)S(1)} %copy-done.1, s32[2048]{0:T(1024)S(1)} %copy-done, s32[16,128]{1,0:T(8,128)S(1)} %bitcast.28, bf16[64,32,256]{2,1,0:T(8,128)(2,1)S(1)} %all_to_all.17.own, bf16[64,32,256]{2,1,0:T(8,128)(2,1)S(1)} %bitcast.27), custom_call_target="tpu_custom_call" | custom-call | tf_op jit(solution)/shard_map/relabel/pallas_call | solution.py:449
  (21 shorter events, 0.1 us)
Async XLA Ops:
  0.0 25.7 %collective-permute-start.3 = (bf16[6912,128]{1,0:T(8,128)(2,1)}, bf16[6912,128]{1,0:T(8,128)(2,1)}, u32[]{:S(2)}, u32[]{:S(2)}) collective-permute-start(bf16[6912,128]{1,0:T(8,128)(2,1)} %bitcast.30), channel_id=1, source_target_pairs={{0,1},{1,0},{2,3},{3,2},{4,5},{5,4},{6,7},{7,6},{8,9},{9,8},{10,11... | collective-permute-start | bytes 5308424 | tf_op jit(solution)/shard_map/ppermute | solution.py:471
  1.4 7.8 %collective-permute-start = (f32[128]{0:T(128)}, f32[128]{0:T(128)S(1)}, u32[]{:S(2)}, u32[]{:S(2)}) collective-permute-start(f32[128]{0:T(128)} %param.24), channel_id=1, source_target_pairs={{0,1},{1,0},{2,3},{3,2},{4,5},{5,4},{6,7},{7,6},{8,9},{9,8},{10,11... | collective-permute-start | bytes 1544 | tf_op jit(solution)/shard_map/ppermute | solution.py:471
  2.4 22.7 %collective-permute-start.2 = (bf16[256,256]{1,0:T(8,128)(2,1)S(1)}, bf16[256,256]{1,0:T(8,128)(2,1)S(1)}, u32[]{:S(2)}, u32[]{:S(2)}) collective-permute-start(bf16[256,256]{1,0:T(8,128)(2,1)S(1)} %get-tuple-element.41), channel_id=1, source_target_pairs={{2,0},{4,2},{6,4},{8,6},{10,8},{12,10},{14,12},{16,14},{18,16},{20... | collective-permute-start | bytes 393224 | tf_op jit(solution)/shard_map/ppermute | solution.py:478
  3.7 21.4 %collective-permute-start.1 = (bf16[256,256]{1,0:T(8,128)(2,1)S(1)}, bf16[256,256]{1,0:T(8,128)(2,1)S(1)}, u32[]{:S(2)}, u32[]{:S(2)}) collective-permute-start(bf16[256,256]{1,0:T(8,128)(2,1)S(1)} %get-tuple-element.42), channel_id=1, source_target_pairs={{0,2},{2,4},{4,6},{6,8},{8,10},{10,12},{12,14},{14,16},{16,18},{18... | collective-permute-start | bytes 393224 | tf_op jit(solution)/shard_map/ppermute | solution.py:477
  9.2 17.1 %copy-start.4 = (f32[128]{0:T(128)}, f32[128]{0:T(128)S(1)}, u32[]{:S(2)}) copy-start(f32[128]{0:T(128)S(1)} %collective-permute-done) | copy-start | bytes 1540
  10.0 36.7 %all-to-all-start = ((s32[64,1,128]{2,1,0:T(1,128)}), s32[64,1,128]{2,1,0:T(1,128)}, u32[]{:S(2)}, u32[]{:S(2)}) async-start(s32[64,1,128]{2,1,0:T(1,128)} %broadcast_in_dim.56), calls=%async_computation | async-start | bytes 65536 | tf_op jit(solution)/shard_map/all_to_all | solution.py:486
  25.1 0.7 copy-start.2
  25.7 0.6 copy-start.3
  46.7 4.0 %collective-permute-start.4 = (bf16[1024,256]{1,0:T(8,128)(2,1)}, bf16[1024,256]{1,0:T(8,128)(2,1)}, u32[]{:S(2)}, u32[]{:S(2)}) collective-permute-start(bf16[1024,256]{1,0:T(8,128)(2,1)} %get-tuple-element.29), channel_id=1, source_target_pairs={{0,1},{1,0},{2,3},{3,2},{4,5},{5,4},{6,7},{7,6},{8,9},{9,8},{10,11... | collective-permute-start | bytes 1572872 | tf_op jit(solution)/shard_map/ppermute | solution.py:471
  48.1 7.7 %collective-permute-start.8 = (bf16[3,256,128]{2,1,0:T(8,128)(2,1)}, bf16[3,256,128]{2,1,0:T(8,128)(2,1)}, u32[]{:S(2)}, u32[]{:S(2)}) collective-permute-start(bf16[3,256,128]{2,1,0:T(8,128)(2,1)} %bitcast.35), channel_id=1, source_target_pairs={{0,1},{1,0},{2,3},{3,2},{4,5},{5,4},{6,7},{7,6},{8,9},{9,8},{10,11... | collective-permute-start | bytes 589832 | tf_op jit(solution)/shard_map/ppermute | solution.py:471
  48.2 2.1 %collective-permute-start.5 = (f32[512]{0:T(512)}, f32[512]{0:T(512)}, u32[]{:S(2)}, u32[]{:S(2)}) collective-permute-start(f32[512]{0:T(512)} %param.35), channel_id=1, source_target_pairs={{0,1},{1,0},{2,3},{3,2},{4,5},{5,4},{6,7},{7,6},{8,9},{9,8},{10,11... | collective-permute-start | bytes 6152 | tf_op jit(solution)/shard_map/ppermute | solution.py:471
  48.6 5.9 %collective-permute-start.9 = (f32[3,128]{1,0:T(4,128)}, f32[3,128]{1,0:T(4,128)}, u32[]{:S(2)}, u32[]{:S(2)}) collective-permute-start(f32[3,128]{1,0:T(4,128)} %qbm.3), channel_id=1, source_target_pairs={{0,1},{1,0},{2,3},{3,2},{4,5},{5,4},{6,7},{7,6},{8,9},{9,8},{10,11... | collective-permute-start | bytes 4616 | tf_op jit(solution)/shard_map/ppermute | solution.py:471
  48.7 30.8 %collective-permute-start.12 = (bf16[256,512]{1,0:T(8,128)(2,1)}, bf16[256,512]{1,0:T(8,128)(2,1)}, u32[]{:S(2)}, u32[]{:S(2)}) collective-permute-start(bf16[256,512]{1,0:T(8,128)(2,1)} %f1m.1), channel_id=1, source_target_pairs={{0,1},{1,0},{2,3},{3,2},{4,5},{5,4},{6,7},{7,6},{8,9},{9,8},{10,11... | collective-permute-start | bytes 786440 | tf_op jit(solution)/shard_map/ppermute | solution.py:471
  50.3 29.3 %collective-permute-start.13 = (bf16[512,256]{1,0:T(8,128)(2,1)}, bf16[512,256]{1,0:T(8,128)(2,1)}, u32[]{:S(2)}, u32[]{:S(2)}) collective-permute-start(bf16[512,256]{1,0:T(8,128)(2,1)} %f2m.1), channel_id=1, source_target_pairs={{0,1},{1,0},{2,3},{3,2},{4,5},{5,4},{6,7},{7,6},{8,9},{9,8},{10,11... | collective-permute-start | bytes 786440 | tf_op jit(solution)/shard_map/ppermute | solution.py:471
  50.7 28.3 %collective-permute-start.6 = (bf16[512,256]{1,0:T(8,128)(2,1)}, bf16[512,256]{1,0:T(8,128)(2,1)}, u32[]{:S(2)}, u32[]{:S(2)}) collective-permute-start(bf16[512,256]{1,0:T(8,128)(2,1)} %get-tuple-element.31), channel_id=1, source_target_pairs={{0,2},{2,4},{4,6},{6,8},{8,10},{10,12},{12,14},{14,16},{16,18},{18... | collective-permute-start | bytes 786440 | tf_op jit(solution)/shard_map/ppermute | solution.py:497
  54.5 24.4 %collective-permute-start.7 = (bf16[512,256]{1,0:T(8,128)(2,1)}, bf16[512,256]{1,0:T(8,128)(2,1)}, u32[]{:S(2)}, u32[]{:S(2)}) collective-permute-start(bf16[512,256]{1,0:T(8,128)(2,1)} %get-tuple-element.32), channel_id=1, source_target_pairs={{2,0},{4,2},{6,4},{8,6},{10,8},{12,10},{14,12},{16,14},{18,16},{20... | collective-permute-start | bytes 786440 | tf_op jit(solution)/shard_map/ppermute | solution.py:498
  79.0 2.0 %collective-permute-start.10 = (bf16[512,256]{1,0:T(8,128)(2,1)}, bf16[512,256]{1,0:T(8,128)(2,1)}, u32[]{:S(2)}, u32[]{:S(2)}) collective-permute-start(bf16[512,256]{1,0:T(8,128)(2,1)} %collective-permute-done.6), channel_id=1, source_target_pairs={{0,1},{1,0},{2,3},{3,2},{4,5},{5,4},{6,7},{7,6},{8,9},{9,8},{10,11... | collective-permute-start | bytes 786440 | tf_op jit(solution)/shard_map/ppermute | solution.py:471
  79.5 1.9 %collective-permute-start.11 = (bf16[512,256]{1,0:T(8,128)(2,1)}, bf16[512,256]{1,0:T(8,128)(2,1)}, u32[]{:S(2)}, u32[]{:S(2)}) collective-permute-start(bf16[512,256]{1,0:T(8,128)(2,1)} %collective-permute-done.7), channel_id=1, source_target_pairs={{0,1},{1,0},{2,3},{3,2},{4,5},{5,4},{6,7},{7,6},{8,9},{9,8},{10,11... | collective-permute-start | bytes 786440 | tf_op jit(solution)/shard_map/ppermute | solution.py:471
  126.5 48.9 %copy-start = (s32[2048]{0:T(1024)S(1)}, s32[2048]{0:T(1024)}, u32[]{:S(2)}) copy-start(s32[2048]{0:T(1024)} %zs.1) | copy-start | bytes 24580
  126.5 48.8 %copy-start.1 = (s32[3]{0:T(128)S(1)}, s32[3]{0:T(128)}, u32[]{:S(2)}) copy-start(s32[3]{0:T(128)} %pad_add_fusion.sc) | copy-start | bytes 40
  171.3 4.1 %collective-permute-start.14 = (bf16[2048,256]{1,0:T(8,128)(2,1)S(1)}, bf16[2048,256]{1,0:T(8,128)(2,1)S(1)}, u32[]{:S(2)}, u32[]{:S(2)}) collective-permute-start(bf16[2048,256]{1,0:T(8,128)(2,1)S(1)} %bitcast.26), channel_id=1, source_target_pairs={{0,1},{1,0},{2,3},{3,2},{4,5},{5,4},{6,7},{7,6},{8,9},{9,8},{10,11... | collective-permute-start | bytes 3145736 | tf_op jit(solution)/shard_map/ppermute | solution.py:471

commit v3 on v2

--- a/solution.py
+++ b/solution.py
@@ -53,7 +53,7 @@
             (cpb, CV.at[0]), (cpg, CV.at[1]), (n1g, CV.at[2]),
         ],
     )
-    wait(started[:4])
+    wait(started[:1])
     lanes = lax.broadcasted_iota(jnp.int32, (RB, 768), 1)
     for b in range(8):
         NB[256 * b : 256 * b + 256, :] = jnp.transpose(NT[:, 256 * b : 256 * b + 256])
@@ -79,6 +79,7 @@
                 pl.ds(pl.multiple_of(256 + 256 * b + 64 * j + 32 * g, 32), 32), :
             ]
 
+    wait(started[1:4])
     for b in range(1024 // RB):
         block(b, OH.at[b % 2])
     wait(started[4:])
@@ -233,15 +234,16 @@
     most_o, QW, QB, PL, sems,
 ):
     g, base, total = sc[0], sc[1], sc[2]
-    wait(
-        copies(
-            sems,
-            [
-                (own, NE.at[:, g]), (oth, NE.at[:, 1 - g]), (qkvm, QW.at[0]), (qkvo, QW.at[1]),
-                (qbm, QB.at[0]), (qbo, QB.at[1]), (plen, PL),
-            ],
-        )
-    )
+    started = copies(
+        sems,
+        [
+            (plen, PL), (own, NE.at[:, g]), (oth, NE.at[:, 1 - g]), (qkvm, QW.at[0]),
+            (qkvo, QW.at[1]), (qbm, QB.at[0]), (qbo, QB.at[1]),
+        ],
+    )
+    wait(started[:1])
+    starts_row, ends_row = patch_rows(PL[...])
+    wait(started[1:])
     block = key_values(NE, KT, V, QW, QB)
     most = lax.fori_loop(0, 8, block, jnp.zeros((8, 256), F32))
     most_o[...] = jnp.broadcast_to(jnp.max(most), (8, 128))
@@ -255,7 +257,6 @@
             pltpu.make_async_copy(q_o.at[at], q_h.at[at], sems.at[12 + qb]),
         )
 
-    starts_row, ends_row = patch_rows(PL[...])
     mask, scores, step = pair_tools()
 
     def q_block(qb, _):
@@ -318,11 +319,12 @@
             (f2m, F2.at[0]), (f2o, F2.at[1]),
         ],
     )
-    wait(started[:11])
-    block = key_values(NE, KT, V, QW, QB)
+    wait(started[8:9])
     starts_row, ends_row = patch_rows(PL[...])
     edge_lo = limits(0, g, base, total, starts_row, ends_row)[2]
     edge_hi = limits(3, g, base, total, starts_row, ends_row)[3]
+    wait(started[:8] + started[9:11])
+    block = key_values(NE, KT, V, QW, QB)
     most = lax.fori_loop(jnp.minimum(edge_lo // 2, 4), 4, block, jnp.zeros((8, 256), F32))
     most = lax.fori_loop(12, jnp.maximum((edge_hi + 1) // 2, 12), block, most)
     key_most = jnp.maximum(jnp.max(most), jnp.max(MI[...]))
@@ -484,16 +486,19 @@
     wanted = jnp.broadcast_to(wanted[:, None, None], (peers, 1, 128))
     wanted, bias_o = lax.optimization_barrier((wanted, bias_o))
     sel = lax.all_to_all(wanted, "pts", split_axis=0, concat_axis=0, tiled=True)
+    qkv_m = jnp.transpose(qkv_w, (1, 0, 2))
+    conv_o, *others = lax.optimization_barrier(
+        (conv_o, swap(qkv_m), swap(qkv_b), swap(fc1_w), swap(fc2_w), swap(fc1_b))
+    )
+    qkv_o, qb_o, fc1_o, fc2_o, b1_o = others
+    weights = (qkv_m, qkv_o, qkv_b, qb_o)
     scalars = jnp.stack([g, me * rows, jnp.int32(rows * peers)])
     section_one, normed, lo_half, hi_half = conv_call(
         scalars, points, low, high, neighbours.T, conv_m, conv_o, conv_b[None], bias_o[None],
         cpe_w, cpe_b[None], cpe_gain[None], norm1_gain[None],
     )
     sel, normed, lo_half, hi_half = lax.optimization_barrier((sel, normed, lo_half, hi_half))
-    qkv_m = jnp.transpose(qkv_w, (1, 0, 2))
-    weights = (qkv_m, swap(qkv_m), qkv_b, swap(qkv_b))
-    fc1_o, fc2_o, b1_o = swap(fc1_w), swap(fc2_w), swap(fc1_b)
-    other, b1_o = lax.optimization_barrier((swap(normed), b1_o))
+    other = swap(normed)
     lo_own = lax.ppermute(lo_half, "pts", forward)
     hi_own = lax.ppermute(hi_half, "pts", backward)
     acc, query, most = near_call(scalars, patch_len[None], pieces(normed), pieces(other), *weights)

time: 176 us -> 179 us (1.017); the launches traced: 178 us -> 178 us
  blocking collectives: 44.8 us -> 42.7 us
    all_to_all x1, blocking collectives: 44.8 us -> 42.7 us  [local(): got = lax.all_to_all(send, 'pts', split_axis=0, concat_axis=0, tiled=True)]
  transfers between devices with their start and end apart: 16 -> 16, of which waited for: 4 -> 4; matrix products, arithmetic and copies ran while one was open for 2% -> 2% of each run, Pallas kernels for 24% -> 25%
where the time goes in v3:
time: 179 us; the launch traced here: 178 us
  Pallas kernels  92.4 us (52%)
  blocking collectives  42.7 us (24%)
  starting transfers between devices  32.1 us (18%)
  local copies, waits for them, and re-layouts  5.1 us (3%)
  waiting for transfers between devices  4.77 us (3%)
    pallas_call x3, Pallas kernels, call(): pl.pallas_call(kernel, out_shape=out_shape, in_specs=[pl.BlockSpec(memory...  89.8 us
    all_to_all x1, blocking collectives, local(): got = lax.all_to_all(send, 'pts', split_axis=0, concat_axis=0, tiled=True)  42.7 us
    all_to_all x1, starting transfers between devices, local(): sel = lax.all_to_all(wanted, 'pts', split_axis=0, concat_axis=0, tiled=True)  15.3 us
    ppermute x11, starting transfers between devices, swap(): return lax.ppermute(x, 'grp', [(0, 1), (1, 0)])  6.59 us
    ppermute x11, waiting for transfers between devices, swap(): return lax.ppermute(x, 'grp', [(0, 1), (1, 0)])  4.76 us
    ppermute x1, starting transfers between devices, local(): low = lax.ppermute(points[rows - 256:], 'pts', forward)  3.99 us
    ppermute x1, starting transfers between devices, local(): lo_own = lax.ppermute(lo_half, 'pts', forward)  3.65 us
  transfers between devices with their start and end apart: 16, of which 4 were waited for; matrix products, arithmetic and copies ran while one was open for 2% of the time, Pallas kernels for 25%

profile of v3, /device:TPU:1, one launch (start us, length us, event | category | flops | bytes accessed | tf_op | source)
XLA Modules:
  0.0 178.1 jit_solution(17090855848500609342)
XLA Ops:
  0.0 1.4 collective-permute-start.3
  1.4 0.5 collective-permute-start.8
  1.9 0.5 collective-permute-start.4
  2.4 1.0 fusion
  3.4 0.8 slice.9
  4.2 0.7 collective-permute-done
  5.0 0.4 collective-permute-start.6
  5.3 0.1 collective-permute-start.7
  5.5 0.6 copy-done.8
  6.1 1.3 collective-permute-start.2
  7.4 4.0 %collective-permute-start.1 = (bf16[256,256]{1,0:T(8,128)(2,1)S(1)}, bf16[256,256]{1,0:T(8,128)(2,1)S(1)}, u32[]{:S(2)}, u32[]{:S(2)}) collective-permute-start(bf16[256,256]{1,0:T(8,128)(2,1)S(1)} %get-tuple-element.50), channel_id=1, source_target_pairs={{0,2},{2,4},{4,6},{6,8},{8,10},{10,12},{12,14},{14,16},{16,18},{18... | collective-permute-start | bytes 393224 | tf_op jit(solution)/shard_map/ppermute | solution.py:479
  11.4 0.7 pad_add_fusion.sc
  12.1 0.1 select_reduce_fusion
  12.1 0.8 broadcast_in_dim.56
  12.9 15.3 %all-to-all-start = ((s32[64,1,128]{2,1,0:T(1,128)}), s32[64,1,128]{2,1,0:T(1,128)}, u32[]{:S(2)}, u32[]{:S(2)}) async-start(s32[64,1,128]{2,1,0:T(1,128)} %broadcast_in_dim.56), calls=%async_computation | async-start | bytes 65536 | tf_op jit(solution)/shard_map/all_to_all | solution.py:488
  28.3 1.3 copy-done.2
  29.6 0.0 copy-done.6
  29.6 0.6 copy-done.7
  30.2 19.9 %conv.1 = (bf16[1024,256]{1,0:T(8,128)(2,1)}, bf16[1024,256]{1,0:T(8,128)(2,1)}, bf16[512,256]{1,0:T(8,128)(2,1)}, bf16[512,256]{1,0:T(8,128)(2,1)}) custom-call(s32[3]{0:T(128)} %pad_add_fusion.sc, bf16[2048,256]{1,0:T(8,128)(2,1)} %pts.1, bf16[256,256]{1,0:T(8,128)(2,1)} %copy-done.7, bf16[256,256]{1,0:T(8,128)(2,1)} %copy-done.6, s32[27,2048]{1,0:T(8,128)} %bitcast.34, ...), custom_call_target="tpu_custom_call" | custom-call | flops 30000001024 | bytes 8000000 | tf_op jit(solution)/shard_map/conv/pallas_call | solution.py:113
  50.2 1.3 collective-permute-start.9
  51.4 3.6 %collective-permute-start.10 = (bf16[512,256]{1,0:T(8,128)(2,1)}, bf16[512,256]{1,0:T(8,128)(2,1)}, u32[]{:S(2)}, u32[]{:S(2)}) collective-permute-start(bf16[512,256]{1,0:T(8,128)(2,1)} %get-tuple-element.35), channel_id=1, source_target_pairs={{0,2},{2,4},{4,6},{6,8},{8,10},{10,12},{12,14},{14,16},{16,18},{18... | collective-permute-start | bytes 786440 | tf_op jit(solution)/shard_map/ppermute | solution.py:502
  55.1 1.3 collective-permute-start.11
  56.4 23.8 %near.1 = (f32[4,2,256,256]{3,2,1,0:T(8,128)}, bf16[1024,256]{1,0:T(8,128)(2,1)}, f32[8,128]{1,0:T(8,128)}) custom-call(s32[3]{0:T(128)} %pad_add_fusion.sc, s32[1,256]{1,0:T(1,128)} %bitcast.43, bf16[32,32,256]{2,1,0:T(8,128)(2,1)} %bitcast.32, bf16[32,32,256]{2,1,0:T(8,128)(2,1)} %bitcast.13.oth, bf16[3,256,128]{2,1,0:T(8,128)(2,1)} %bitcast.36, ...), custom_call_target="tpu_custom_call" | custom-call | flops 20000000000 | bytes 8000000 | tf_op jit(solution)/shard_map/near/pallas_call | solution.py:113
  80.3 0.4 collective-permute-start.12
  80.6 0.2 collective-permute-start.13
  80.9 1.4 collective-permute-done.12
  82.2 0.4 collective-permute-done.13
  82.6 46.1 %far.1 = bf16[2048,256]{1,0:T(8,128)(2,1)} custom-call(s32[3]{0:T(128)} %pad_add_fusion.sc, s32[64,1,128]{2,1,0:T(1,128)} %all-to-all-done.sel, s32[1,256]{1,0:T(1,128)} %bitcast.44, bf16[32,32,256]{2,1,0:T(8,128)(2,1)} %bitcast.33, bf16[32,32,256]{2,1,0:T(8,128)(2,1)} %bitcast.13.oth, bf16[16,32,256]{2,1,0:T(8,128)(2,1)} %bitcast.14.lo_own, ...), custom_call_target="tpu_custom_call" | custom-call | flops 20000000000 | bytes 8000000 | tf_op jit(solution)/shard_map/far/pallas_call | solution.py:113
  128.7 42.7 %all_to_all.17.own = bf16[64,32,256]{2,1,0:T(8,128)(2,1)S(1)} all-to-all(bf16[64,32,256]{2,1,0:T(8,128)(2,1)} %bitcast.29), channel_id=1, replica_groups=mesh['pts'=64,'grp'=2] {'pts'}, dimensions={0} | all-to-all | bytes 2097152 | tf_op jit(solution)/shard_map/all_to_all | solution.py:513
  171.4 1.8 collective-permute-start.14
  173.2 2.3 %collective-permute-done.14 = bf16[2048,256]{1,0:T(8,128)(2,1)S(1)} collective-permute-done((bf16[2048,256]{1,0:T(8,128)(2,1)S(1)}, bf16[2048,256]{1,0:T(8,128)(2,1)S(1)}, u32[]{:S(2)}, u32[]{:S(2)}) %collective-permute-start.14) | collective-permute-done | bytes 1048608 | tf_op jit(solution)/shard_map/ppermute | solution.py:473
  175.5 2.6 %relabel.1 = bf16[2048,256]{1,0:T(8,128)(2,1)} custom-call(s32[3]{0:T(128)S(1)} %copy-done.1, s32[2048]{0:T(1024)S(1)} %copy-done, s32[16,128]{1,0:T(8,128)S(1)} %bitcast.28, bf16[64,32,256]{2,1,0:T(8,128)(2,1)S(1)} %all_to_all.17.own, bf16[64,32,256]{2,1,0:T(8,128)(2,1)S(1)} %bitcast.27), custom_call_target="tpu_custom_call" | custom-call | tf_op jit(solution)/shard_map/relabel/pallas_call | solution.py:451
  (31 shorter events, 0.1 us)
Async XLA Ops:
  0.0 28.2 %collective-permute-start.3 = (bf16[6912,128]{1,0:T(8,128)(2,1)}, bf16[6912,128]{1,0:T(8,128)(2,1)S(1)}, u32[]{:S(2)}, u32[]{:S(2)}) collective-permute-start(bf16[6912,128]{1,0:T(8,128)(2,1)} %bitcast.30), channel_id=1, source_target_pairs={{0,1},{1,0},{2,3},{3,2},{4,5},{5,4},{6,7},{7,6},{8,9},{9,8},{10,11... | collective-permute-start | bytes 5308424 | tf_op jit(solution)/shard_map/ppermute | solution.py:473
  1.4 3.5 %collective-permute-start = (f32[128]{0:T(128)}, f32[128]{0:T(128)S(1)}, u32[]{:S(2)}, u32[]{:S(2)}) collective-permute-start(f32[128]{0:T(128)} %param.24), channel_id=1, source_target_pairs={{0,1},{1,0},{2,3},{3,2},{4,5},{5,4},{6,7},{7,6},{8,9},{9,8},{10,11... | collective-permute-start | bytes 1544 | tf_op jit(solution)/shard_map/ppermute | solution.py:473
  1.4 4.1 %collective-permute-start.8 = (f32[512]{0:T(512)}, f32[512]{0:T(512)S(1)}, u32[]{:S(2)}, u32[]{:S(2)}) collective-permute-start(f32[512]{0:T(512)} %param.35), channel_id=1, source_target_pairs={{0,1},{1,0},{2,3},{3,2},{4,5},{5,4},{6,7},{7,6},{8,9},{9,8},{10,11... | collective-permute-start | bytes 6152 | tf_op jit(solution)/shard_map/ppermute | solution.py:473
  1.9 3.4 %collective-permute-start.5 = (f32[3,128]{1,0:T(4,128)}, f32[3,128]{1,0:T(4,128)}, u32[]{:S(2)}, u32[]{:S(2)}) collective-permute-start(f32[3,128]{1,0:T(4,128)} %qbm.3), channel_id=1, source_target_pairs={{0,1},{1,0},{2,3},{3,2},{4,5},{5,4},{6,7},{7,6},{8,9},{9,8},{10,11... | collective-permute-start | bytes 4616 | tf_op jit(solution)/shard_map/ppermute | solution.py:473
  1.9 5.4 %collective-permute-start.4 = (bf16[3,256,128]{2,1,0:T(8,128)(2,1)}, bf16[3,256,128]{2,1,0:T(8,128)(2,1)S(1)}, u32[]{:S(2)}, u32[]{:S(2)}) collective-permute-start(bf16[3,256,128]{2,1,0:T(8,128)(2,1)} %bitcast.35), channel_id=1, source_target_pairs={{0,1},{1,0},{2,3},{3,2},{4,5},{5,4},{6,7},{7,6},{8,9},{9,8},{10,11... | collective-permute-start | bytes 589832 | tf_op jit(solution)/shard_map/ppermute | solution.py:473
  5.0 24.7 %copy-start.9 = (f32[128]{0:T(128)}, f32[128]{0:T(128)S(1)}, u32[]{:S(2)}) copy-start(f32[128]{0:T(128)S(1)} %collective-permute-done) | copy-start | bytes 1540
  5.0 23.2 %collective-permute-start.6 = (bf16[256,512]{1,0:T(8,128)(2,1)}, bf16[256,512]{1,0:T(8,128)(2,1)S(1)}, u32[]{:S(2)}, u32[]{:S(2)}) collective-permute-start(bf16[256,512]{1,0:T(8,128)(2,1)} %f1m.1), channel_id=1, source_target_pairs={{0,1},{1,0},{2,3},{3,2},{4,5},{5,4},{6,7},{7,6},{8,9},{9,8},{10,11... | collective-permute-start | bytes 786440 | tf_op jit(solution)/shard_map/ppermute | solution.py:473
  5.3 22.9 %collective-permute-start.7 = (bf16[512,256]{1,0:T(8,128)(2,1)}, bf16[512,256]{1,0:T(8,128)(2,1)S(1)}, u32[]{:S(2)}, u32[]{:S(2)}) collective-permute-start(bf16[512,256]{1,0:T(8,128)(2,1)} %f2m.1), channel_id=1, source_target_pairs={{0,1},{1,0},{2,3},{3,2},{4,5},{5,4},{6,7},{7,6},{8,9},{9,8},{10,11... | collective-permute-start | bytes 786440 | tf_op jit(solution)/shard_map/ppermute | solution.py:473
  5.5 0.6 copy-start.8
  6.1 22.2 %collective-permute-start.2 = (bf16[256,256]{1,0:T(8,128)(2,1)S(1)}, bf16[256,256]{1,0:T(8,128)(2,1)S(1)}, u32[]{:S(2)}, u32[]{:S(2)}) collective-permute-start(bf16[256,256]{1,0:T(8,128)(2,1)S(1)} %get-tuple-element.49), channel_id=1, source_target_pairs={{2,0},{4,2},{6,4},{8,6},{10,8},{12,10},{14,12},{16,14},{18,16},{20... | collective-permute-start | bytes 393224 | tf_op jit(solution)/shard_map/ppermute | solution.py:480
  7.4 22.2 %copy-start.5 = (bf16[3,256,128]{2,1,0:T(8,128)(2,1)}, bf16[3,256,128]{2,1,0:T(8,128)(2,1)S(1)}, u32[]{:S(2)}) copy-start(bf16[3,256,128]{2,1,0:T(8,128)(2,1)S(1)} %collective-permute-done.4.qkvo) | copy-start | bytes 589828
  7.4 20.9 %collective-permute-start.1 = (bf16[256,256]{1,0:T(8,128)(2,1)S(1)}, bf16[256,256]{1,0:T(8,128)(2,1)S(1)}, u32[]{:S(2)}, u32[]{:S(2)}) collective-permute-start(bf16[256,256]{1,0:T(8,128)(2,1)S(1)} %get-tuple-element.50), channel_id=1, source_target_pairs={{0,2},{2,4},{4,6},{6,8},{8,10},{10,12},{12,14},{14,16},{16,18},{18... | collective-permute-start | bytes 393224 | tf_op jit(solution)/shard_map/ppermute | solution.py:479
  12.9 37.2 %all-to-all-start = ((s32[64,1,128]{2,1,0:T(1,128)}), s32[64,1,128]{2,1,0:T(1,128)}, u32[]{:S(2)}, u32[]{:S(2)}) async-start(s32[64,1,128]{2,1,0:T(1,128)} %broadcast_in_dim.56), calls=%async_computation | async-start | bytes 65536 | tf_op jit(solution)/shard_map/all_to_all | solution.py:488
  28.2 1.4 copy-start.3
  28.2 1.4 copy-start.4
  28.2 1.4 copy-start.2
  28.3 1.4 copy-start.6
  29.6 0.7 copy-start.7
  50.2 6.2 %collective-permute-start.9 = (bf16[1024,256]{1,0:T(8,128)(2,1)}, bf16[1024,256]{1,0:T(8,128)(2,1)}, u32[]{:S(2)}, u32[]{:S(2)}) collective-permute-start(bf16[1024,256]{1,0:T(8,128)(2,1)} %get-tuple-element.34), channel_id=1, source_target_pairs={{0,1},{1,0},{2,3},{3,2},{4,5},{5,4},{6,7},{7,6},{8,9},{9,8},{10,11... | collective-permute-start | bytes 1572872 | tf_op jit(solution)/shard_map/ppermute | solution.py:473
  51.4 28.8 %collective-permute-start.10 = (bf16[512,256]{1,0:T(8,128)(2,1)}, bf16[512,256]{1,0:T(8,128)(2,1)}, u32[]{:S(2)}, u32[]{:S(2)}) collective-permute-start(bf16[512,256]{1,0:T(8,128)(2,1)} %get-tuple-element.35), channel_id=1, source_target_pairs={{0,2},{2,4},{4,6},{6,8},{8,10},{10,12},{12,14},{14,16},{16,18},{18... | collective-permute-start | bytes 786440 | tf_op jit(solution)/shard_map/ppermute | solution.py:502
  55.1 25.2 %collective-permute-start.11 = (bf16[512,256]{1,0:T(8,128)(2,1)}, bf16[512,256]{1,0:T(8,128)(2,1)}, u32[]{:S(2)}, u32[]{:S(2)}) collective-permute-start(bf16[512,256]{1,0:T(8,128)(2,1)} %get-tuple-element.36), channel_id=1, source_target_pairs={{2,0},{4,2},{6,4},{8,6},{10,8},{12,10},{14,12},{16,14},{18,16},{20... | collective-permute-start | bytes 786440 | tf_op jit(solution)/shard_map/ppermute | solution.py:503
  80.3 2.0 %collective-permute-start.12 = (bf16[512,256]{1,0:T(8,128)(2,1)}, bf16[512,256]{1,0:T(8,128)(2,1)}, u32[]{:S(2)}, u32[]{:S(2)}) collective-permute-start(bf16[512,256]{1,0:T(8,128)(2,1)} %collective-permute-done.10), channel_id=1, source_target_pairs={{0,1},{1,0},{2,3},{3,2},{4,5},{5,4},{6,7},{7,6},{8,9},{9,8},{10,11... | collective-permute-start | bytes 786440 | tf_op jit(solution)/shard_map/ppermute | solution.py:473
  80.6 2.0 %collective-permute-start.13 = (bf16[512,256]{1,0:T(8,128)(2,1)}, bf16[512,256]{1,0:T(8,128)(2,1)}, u32[]{:S(2)}, u32[]{:S(2)}) collective-permute-start(bf16[512,256]{1,0:T(8,128)(2,1)} %collective-permute-done.11), channel_id=1, source_target_pairs={{0,1},{1,0},{2,3},{3,2},{4,5},{5,4},{6,7},{7,6},{8,9},{9,8},{10,11... | collective-permute-start | bytes 786440 | tf_op jit(solution)/shard_map/ppermute | solution.py:473
  128.7 46.8 %copy-start = (s32[2048]{0:T(1024)S(1)}, s32[2048]{0:T(1024)}, u32[]{:S(2)}) copy-start(s32[2048]{0:T(1024)} %zs.1) | copy-start | bytes 24580
  128.7 46.8 %copy-start.1 = (s32[3]{0:T(128)S(1)}, s32[3]{0:T(128)}, u32[]{:S(2)}) copy-start(s32[3]{0:T(128)} %pad_add_fusion.sc) | copy-start | bytes 40
  171.4 4.0 %collective-permute-start.14 = (bf16[2048,256]{1,0:T(8,128)(2,1)S(1)}, bf16[2048,256]{1,0:T(8,128)(2,1)S(1)}, u32[]{:S(2)}, u32[]{:S(2)}) collective-permute-start(bf16[2048,256]{1,0:T(8,128)(2,1)S(1)} %bitcast.26), channel_id=1, source_target_pairs={{0,1},{1,0},{2,3},{3,2},{4,5},{5,4},{6,7},{7,6},{8,9},{9,8},{10,11... | collective-permute-start | bytes 3145736 | tf_op jit(solution)/shard_map/ppermute | solution.py:473

commit v4 on v3

--- a/solution.py
+++ b/solution.py
@@ -133,23 +133,21 @@
 
 
 def key_values(NE, KT, V, QW, QB):
-    wkt = [jnp.transpose(QW[h, 1]) for h in range(2)]
-    bkc = [jnp.transpose(jnp.broadcast_to(QB[h, 1:2, :], (8, 128)))[:, :1] for h in range(2)]
+    wkt = jnp.concatenate([jnp.transpose(QW[h, 1]) for h in range(2)], axis=0)
+    bkc = jnp.concatenate(
+        [jnp.transpose(jnp.broadcast_to(QB[h, 1:2, :], (8, 128)))[:, :1] for h in range(2)], axis=0
+    )
     wv = jnp.concatenate([QW[0, 2], QW[1, 2]], axis=1)
     bv = jnp.concatenate([QB[0, 2:3, :], QB[1, 2:3, :]], axis=1)
 
     def block(i, most):
         r0 = pl.multiple_of(i * 256, 256)
         rows = NE[pl.ds(4 * i, 4)].reshape(256, 256)
-        for h in range(2):
-            kt = (
-                lax.dot_general(
-                    wkt[h], rows, (((1,), (1,)), ((), ())), preferred_element_type=F32
-                )
-                + bkc[h]
-            )
-            most = jnp.maximum(most, jnp.sum((kt * kt).reshape(8, 16, 256), axis=1))
-            KT[128 * h : 128 * h + 128, pl.ds(r0, 256)] = kt.astype(BF)
+        kt = (
+            lax.dot_general(wkt, rows, (((1,), (1,)), ((), ())), preferred_element_type=F32) + bkc
+        )
+        most = jnp.maximum(most, jnp.sum((kt * kt).reshape(16, 16, 256), axis=1))
+        KT[:, pl.ds(r0, 256)] = kt.astype(BF)
         V[pl.ds(r0, 256), :] = (jnp.dot(rows, wv, preferred_element_type=F32) + bv).astype(BF)
         return most
 
@@ -245,7 +243,7 @@
     starts_row, ends_row = patch_rows(PL[...])
     wait(started[1:])
     block = key_values(NE, KT, V, QW, QB)
-    most = lax.fori_loop(0, 8, block, jnp.zeros((8, 256), F32))
+    most = lax.fori_loop(0, 8, block, jnp.zeros((16, 256), F32))
     most_o[...] = jnp.broadcast_to(jnp.max(most), (8, 128))
     leave = pltpu.make_async_copy(most_o, most_h, sems.at[7])
     leave.start()
@@ -325,7 +323,7 @@
     edge_hi = limits(3, g, base, total, starts_row, ends_row)[3]
     wait(started[:8] + started[9:11])
     block = key_values(NE, KT, V, QW, QB)
-    most = lax.fori_loop(jnp.minimum(edge_lo // 2, 4), 4, block, jnp.zeros((8, 256), F32))
+    most = lax.fori_loop(jnp.minimum(edge_lo // 2, 4), 4, block, jnp.zeros((16, 256), F32))
     most = lax.fori_loop(12, jnp.maximum((edge_hi + 1) // 2, 12), block, most)
     key_most = jnp.maximum(jnp.max(most), jnp.max(MI[...]))
     mask, scores, step = pair_tools()
@@ -344,7 +342,7 @@
     @pl.when(jnp.logical_not(calm))
     def _():
         wait(copies(sems.at[24:26], [(own, NE.at[16:48, g]), (oth, NE.at[16:48, 1 - g])]))
-        lax.fori_loop(4, 12, block, jnp.zeros((8, 256), F32))
+        lax.fori_loop(4, 12, block, jnp.zeros((16, 256), F32))
 
     wait(started[11:])
 

time: 179 us -> 176 us (0.983)
  Pallas kernels: 92.4 us -> 90.2 us
    pallas_call x3, Pallas kernels: 89.8 us -> 87.6 us  [call(): pl.pallas_call(kernel, out_shape=out_shape, in_specs=[pl.BlockSpec(memory...]
  transfers between devices with their start and end apart: 16 -> 16, of which waited for: 4 -> 4; matrix products, arithmetic and copies ran while one was open for 2% -> 2% of each run, Pallas kernels for 25% -> 24%
where the time goes in v4:
time: 176 us
  Pallas kernels  90.2 us (51%)
  blocking collectives  42.7 us (24%)
  starting transfers between devices  32.1 us (18%)
  local copies, waits for them, and re-layouts  5.1 us (3%)
  waiting for transfers between devices  4.77 us (3%)
    pallas_call x3, Pallas kernels, call(): pl.pallas_call(kernel, out_shape=out_shape, in_specs=[pl.BlockSpec(memory...  87.6 us
    all_to_all x1, blocking collectives, local(): got = lax.all_to_all(send, 'pts', split_axis=0, concat_axis=0, tiled=True)  42.7 us
    all_to_all x1, starting transfers between devices, local(): sel = lax.all_to_all(wanted, 'pts', split_axis=0, concat_axis=0, tiled=True)  15.3 us
    ppermute x11, starting transfers between devices, swap(): return lax.ppermute(x, 'grp', [(0, 1), (1, 0)])  6.58 us
    ppermute x11, waiting for transfers between devices, swap(): return lax.ppermute(x, 'grp', [(0, 1), (1, 0)])  4.76 us
    ppermute x1, starting transfers between devices, local(): low = lax.ppermute(points[rows - 256:], 'pts', forward)  3.99 us
    ppermute x1, starting transfers between devices, local(): lo_own = lax.ppermute(lo_half, 'pts', forward)  3.65 us
  transfers between devices with their start and end apart: 16, of which 4 were waited for; matrix products, arithmetic and copies ran while one was open for 2% of the time, Pallas kernels for 24%

profile of v4, /device:TPU:1, one launch (start us, length us, event | category | flops | bytes accessed | tf_op | source)
XLA Modules:
  0.0 175.8 jit_solution(13329976889122338722)
XLA Ops:
  0.0 1.4 collective-permute-start.3
  1.4 0.5 collective-permute-start.8
  1.9 0.5 collective-permute-start.4
  2.4 1.0 fusion
  3.4 0.8 slice.9
  4.2 0.7 collective-permute-done
  5.0 0.4 collective-permute-start.6
  5.3 0.1 collective-permute-start.7
  5.5 0.6 copy-done.8
  6.1 1.3 collective-permute-start.2
  7.4 4.0 %collective-permute-start.1 = (bf16[256,256]{1,0:T(8,128)(2,1)S(1)}, bf16[256,256]{1,0:T(8,128)(2,1)S(1)}, u32[]{:S(2)}, u32[]{:S(2)}) collective-permute-start(bf16[256,256]{1,0:T(8,128)(2,1)S(1)} %get-tuple-element.50), channel_id=1, source_target_pairs={{0,2},{2,4},{4,6},{6,8},{8,10},{10,12},{12,14},{14,16},{16,18},{18... | collective-permute-start | bytes 393224 | tf_op jit(solution)/shard_map/ppermute | solution.py:477
  11.4 0.7 pad_add_fusion.sc
  12.1 0.1 select_reduce_fusion
  12.1 0.8 broadcast_in_dim.56
  12.9 15.3 %all-to-all-start = ((s32[64,1,128]{2,1,0:T(1,128)}), s32[64,1,128]{2,1,0:T(1,128)}, u32[]{:S(2)}, u32[]{:S(2)}) async-start(s32[64,1,128]{2,1,0:T(1,128)} %broadcast_in_dim.56), calls=%async_computation | async-start | bytes 65536 | tf_op jit(solution)/shard_map/all_to_all | solution.py:486
  28.3 1.3 copy-done.2
  29.6 0.0 copy-done.6
  29.6 0.6 copy-done.7
  30.2 19.9 %conv.1 = (bf16[1024,256]{1,0:T(8,128)(2,1)}, bf16[1024,256]{1,0:T(8,128)(2,1)}, bf16[512,256]{1,0:T(8,128)(2,1)}, bf16[512,256]{1,0:T(8,128)(2,1)}) custom-call(s32[3]{0:T(128)} %pad_add_fusion.sc, bf16[2048,256]{1,0:T(8,128)(2,1)} %pts.1, bf16[256,256]{1,0:T(8,128)(2,1)} %copy-done.7, bf16[256,256]{1,0:T(8,128)(2,1)} %copy-done.6, s32[27,2048]{1,0:T(8,128)} %bitcast.34, ...), custom_call_target="tpu_custom_call" | custom-call | flops 30000001024 | bytes 8000000 | tf_op jit(solution)/shard_map/conv/pallas_call | solution.py:113
  50.2 1.3 collective-permute-start.9
  51.4 3.6 %collective-permute-start.10 = (bf16[512,256]{1,0:T(8,128)(2,1)}, bf16[512,256]{1,0:T(8,128)(2,1)}, u32[]{:S(2)}, u32[]{:S(2)}) collective-permute-start(bf16[512,256]{1,0:T(8,128)(2,1)} %get-tuple-element.35), channel_id=1, source_target_pairs={{0,2},{2,4},{4,6},{6,8},{8,10},{10,12},{12,14},{14,16},{16,18},{18... | collective-permute-start | bytes 786440 | tf_op jit(solution)/shard_map/ppermute | solution.py:500
  55.1 1.3 collective-permute-start.11
  56.4 23.0 %near.1 = (f32[4,2,256,256]{3,2,1,0:T(8,128)}, bf16[1024,256]{1,0:T(8,128)(2,1)}, f32[8,128]{1,0:T(8,128)}) custom-call(s32[3]{0:T(128)} %pad_add_fusion.sc, s32[1,256]{1,0:T(1,128)} %bitcast.43, bf16[32,32,256]{2,1,0:T(8,128)(2,1)} %bitcast.32, bf16[32,32,256]{2,1,0:T(8,128)(2,1)} %bitcast.13.oth, bf16[3,256,128]{2,1,0:T(8,128)(2,1)} %bitcast.36, ...), custom_call_target="tpu_custom_call" | custom-call | flops 20000000000 | bytes 8000000 | tf_op jit(solution)/shard_map/near/pallas_call | solution.py:113
  79.4 0.1 collective-permute-start.12
  79.5 0.5 collective-permute-start.13
  80.0 1.4 collective-permute-done.12
  81.3 0.4 collective-permute-done.13
  81.7 44.7 %far.1 = bf16[2048,256]{1,0:T(8,128)(2,1)} custom-call(s32[3]{0:T(128)} %pad_add_fusion.sc, s32[64,1,128]{2,1,0:T(1,128)} %all-to-all-done.sel, s32[1,256]{1,0:T(1,128)} %bitcast.44, bf16[32,32,256]{2,1,0:T(8,128)(2,1)} %bitcast.33, bf16[32,32,256]{2,1,0:T(8,128)(2,1)} %bitcast.13.oth, bf16[16,32,256]{2,1,0:T(8,128)(2,1)} %bitcast.14.lo_own, ...), custom_call_target="tpu_custom_call" | custom-call | flops 20000000000 | bytes 8000000 | tf_op jit(solution)/shard_map/far/pallas_call | solution.py:113
  126.5 42.7 %all_to_all.17.own = bf16[64,32,256]{2,1,0:T(8,128)(2,1)S(1)} all-to-all(bf16[64,32,256]{2,1,0:T(8,128)(2,1)} %bitcast.29), channel_id=1, replica_groups=mesh['pts'=64,'grp'=2] {'pts'}, dimensions={0} | all-to-all | bytes 2097152 | tf_op jit(solution)/shard_map/all_to_all | solution.py:511
  169.2 1.8 collective-permute-start.14
  170.9 2.3 %collective-permute-done.14 = bf16[2048,256]{1,0:T(8,128)(2,1)S(1)} collective-permute-done((bf16[2048,256]{1,0:T(8,128)(2,1)S(1)}, bf16[2048,256]{1,0:T(8,128)(2,1)S(1)}, u32[]{:S(2)}, u32[]{:S(2)}) %collective-permute-start.14) | collective-permute-done | bytes 1048608 | tf_op jit(solution)/shard_map/ppermute | solution.py:471
  173.2 2.6 %relabel.1 = bf16[2048,256]{1,0:T(8,128)(2,1)} custom-call(s32[3]{0:T(128)S(1)} %copy-done.1, s32[2048]{0:T(1024)S(1)} %copy-done, s32[16,128]{1,0:T(8,128)S(1)} %bitcast.28, bf16[64,32,256]{2,1,0:T(8,128)(2,1)S(1)} %all_to_all.17.own, bf16[64,32,256]{2,1,0:T(8,128)(2,1)S(1)} %bitcast.27), custom_call_target="tpu_custom_call" | custom-call | tf_op jit(solution)/shard_map/relabel/pallas_call | solution.py:449
  (31 shorter events, 0.1 us)
Async XLA Ops:
  0.0 28.2 %collective-permute-start.3 = (bf16[6912,128]{1,0:T(8,128)(2,1)}, bf16[6912,128]{1,0:T(8,128)(2,1)S(1)}, u32[]{:S(2)}, u32[]{:S(2)}) collective-permute-start(bf16[6912,128]{1,0:T(8,128)(2,1)} %bitcast.30), channel_id=1, source_target_pairs={{0,1},{1,0},{2,3},{3,2},{4,5},{5,4},{6,7},{7,6},{8,9},{9,8},{10,11... | collective-permute-start | bytes 5308424 | tf_op jit(solution)/shard_map/ppermute | solution.py:471
  1.4 3.5 %collective-permute-start = (f32[128]{0:T(128)}, f32[128]{0:T(128)S(1)}, u32[]{:S(2)}, u32[]{:S(2)}) collective-permute-start(f32[128]{0:T(128)} %param.24), channel_id=1, source_target_pairs={{0,1},{1,0},{2,3},{3,2},{4,5},{5,4},{6,7},{7,6},{8,9},{9,8},{10,11... | collective-permute-start | bytes 1544 | tf_op jit(solution)/shard_map/ppermute | solution.py:471
  1.4 4.1 %collective-permute-start.8 = (f32[512]{0:T(512)}, f32[512]{0:T(512)S(1)}, u32[]{:S(2)}, u32[]{:S(2)}) collective-permute-start(f32[512]{0:T(512)} %param.35), channel_id=1, source_target_pairs={{0,1},{1,0},{2,3},{3,2},{4,5},{5,4},{6,7},{7,6},{8,9},{9,8},{10,11... | collective-permute-start | bytes 6152 | tf_op jit(solution)/shard_map/ppermute | solution.py:471
  1.9 3.4 %collective-permute-start.5 = (f32[3,128]{1,0:T(4,128)}, f32[3,128]{1,0:T(4,128)}, u32[]{:S(2)}, u32[]{:S(2)}) collective-permute-start(f32[3,128]{1,0:T(4,128)} %qbm.3), channel_id=1, source_target_pairs={{0,1},{1,0},{2,3},{3,2},{4,5},{5,4},{6,7},{7,6},{8,9},{9,8},{10,11... | collective-permute-start | bytes 4616 | tf_op jit(solution)/shard_map/ppermute | solution.py:471
  1.9 5.4 %collective-permute-start.4 = (bf16[3,256,128]{2,1,0:T(8,128)(2,1)}, bf16[3,256,128]{2,1,0:T(8,128)(2,1)S(1)}, u32[]{:S(2)}, u32[]{:S(2)}) collective-permute-start(bf16[3,256,128]{2,1,0:T(8,128)(2,1)} %bitcast.35), channel_id=1, source_target_pairs={{0,1},{1,0},{2,3},{3,2},{4,5},{5,4},{6,7},{7,6},{8,9},{9,8},{10,11... | collective-permute-start | bytes 589832 | tf_op jit(solution)/shard_map/ppermute | solution.py:471
  5.0 24.7 %copy-start.9 = (f32[128]{0:T(128)}, f32[128]{0:T(128)S(1)}, u32[]{:S(2)}) copy-start(f32[128]{0:T(128)S(1)} %collective-permute-done) | copy-start | bytes 1540
  5.0 23.2 %collective-permute-start.6 = (bf16[256,512]{1,0:T(8,128)(2,1)}, bf16[256,512]{1,0:T(8,128)(2,1)S(1)}, u32[]{:S(2)}, u32[]{:S(2)}) collective-permute-start(bf16[256,512]{1,0:T(8,128)(2,1)} %f1m.1), channel_id=1, source_target_pairs={{0,1},{1,0},{2,3},{3,2},{4,5},{5,4},{6,7},{7,6},{8,9},{9,8},{10,11... | collective-permute-start | bytes 786440 | tf_op jit(solution)/shard_map/ppermute | solution.py:471
  5.3 22.9 %collective-permute-start.7 = (bf16[512,256]{1,0:T(8,128)(2,1)}, bf16[512,256]{1,0:T(8,128)(2,1)S(1)}, u32[]{:S(2)}, u32[]{:S(2)}) collective-permute-start(bf16[512,256]{1,0:T(8,128)(2,1)} %f2m.1), channel_id=1, source_target_pairs={{0,1},{1,0},{2,3},{3,2},{4,5},{5,4},{6,7},{7,6},{8,9},{9,8},{10,11... | collective-permute-start | bytes 786440 | tf_op jit(solution)/shard_map/ppermute | solution.py:471
  5.5 0.6 copy-start.8
  6.1 22.2 %collective-permute-start.2 = (bf16[256,256]{1,0:T(8,128)(2,1)S(1)}, bf16[256,256]{1,0:T(8,128)(2,1)S(1)}, u32[]{:S(2)}, u32[]{:S(2)}) collective-permute-start(bf16[256,256]{1,0:T(8,128)(2,1)S(1)} %get-tuple-element.49), channel_id=1, source_target_pairs={{2,0},{4,2},{6,4},{8,6},{10,8},{12,10},{14,12},{16,14},{18,16},{20... | collective-permute-start | bytes 393224 | tf_op jit(solution)/shard_map/ppermute | solution.py:478
  7.4 22.2 %copy-start.5 = (bf16[3,256,128]{2,1,0:T(8,128)(2,1)}, bf16[3,256,128]{2,1,0:T(8,128)(2,1)S(1)}, u32[]{:S(2)}) copy-start(bf16[3,256,128]{2,1,0:T(8,128)(2,1)S(1)} %collective-permute-done.4.qkvo) | copy-start | bytes 589828
  7.4 20.9 %collective-permute-start.1 = (bf16[256,256]{1,0:T(8,128)(2,1)S(1)}, bf16[256,256]{1,0:T(8,128)(2,1)S(1)}, u32[]{:S(2)}, u32[]{:S(2)}) collective-permute-start(bf16[256,256]{1,0:T(8,128)(2,1)S(1)} %get-tuple-element.50), channel_id=1, source_target_pairs={{0,2},{2,4},{4,6},{6,8},{8,10},{10,12},{12,14},{14,16},{16,18},{18... | collective-permute-start | bytes 393224 | tf_op jit(solution)/shard_map/ppermute | solution.py:477
  12.9 37.2 %all-to-all-start = ((s32[64,1,128]{2,1,0:T(1,128)}), s32[64,1,128]{2,1,0:T(1,128)}, u32[]{:S(2)}, u32[]{:S(2)}) async-start(s32[64,1,128]{2,1,0:T(1,128)} %broadcast_in_dim.56), calls=%async_computation | async-start | bytes 65536 | tf_op jit(solution)/shard_map/all_to_all | solution.py:486
  28.2 1.4 copy-start.3
  28.2 1.4 copy-start.4
  28.2 1.4 copy-start.2
  28.3 1.4 copy-start.6
  29.6 0.7 copy-start.7
  50.2 6.2 %collective-permute-start.9 = (bf16[1024,256]{1,0:T(8,128)(2,1)}, bf16[1024,256]{1,0:T(8,128)(2,1)}, u32[]{:S(2)}, u32[]{:S(2)}) collective-permute-start(bf16[1024,256]{1,0:T(8,128)(2,1)} %get-tuple-element.34), channel_id=1, source_target_pairs={{0,1},{1,0},{2,3},{3,2},{4,5},{5,4},{6,7},{7,6},{8,9},{9,8},{10,11... | collective-permute-start | bytes 1572872 | tf_op jit(solution)/shard_map/ppermute | solution.py:471
  51.4 27.9 %collective-permute-start.10 = (bf16[512,256]{1,0:T(8,128)(2,1)}, bf16[512,256]{1,0:T(8,128)(2,1)}, u32[]{:S(2)}, u32[]{:S(2)}) collective-permute-start(bf16[512,256]{1,0:T(8,128)(2,1)} %get-tuple-element.35), channel_id=1, source_target_pairs={{0,2},{2,4},{4,6},{6,8},{8,10},{10,12},{12,14},{14,16},{16,18},{18... | collective-permute-start | bytes 786440 | tf_op jit(solution)/shard_map/ppermute | solution.py:500
  55.1 24.3 %collective-permute-start.11 = (bf16[512,256]{1,0:T(8,128)(2,1)}, bf16[512,256]{1,0:T(8,128)(2,1)}, u32[]{:S(2)}, u32[]{:S(2)}) collective-permute-start(bf16[512,256]{1,0:T(8,128)(2,1)} %get-tuple-element.36), channel_id=1, source_target_pairs={{2,0},{4,2},{6,4},{8,6},{10,8},{12,10},{14,12},{16,14},{18,16},{20... | collective-permute-start | bytes 786440 | tf_op jit(solution)/shard_map/ppermute | solution.py:501
  79.4 2.0 %collective-permute-start.12 = (bf16[512,256]{1,0:T(8,128)(2,1)}, bf16[512,256]{1,0:T(8,128)(2,1)}, u32[]{:S(2)}, u32[]{:S(2)}) collective-permute-start(bf16[512,256]{1,0:T(8,128)(2,1)} %collective-permute-done.10), channel_id=1, source_target_pairs={{0,1},{1,0},{2,3},{3,2},{4,5},{5,4},{6,7},{7,6},{8,9},{9,8},{10,11... | collective-permute-start | bytes 786440 | tf_op jit(solution)/shard_map/ppermute | solution.py:471
  79.5 2.2 %collective-permute-start.13 = (bf16[512,256]{1,0:T(8,128)(2,1)}, bf16[512,256]{1,0:T(8,128)(2,1)}, u32[]{:S(2)}, u32[]{:S(2)}) collective-permute-start(bf16[512,256]{1,0:T(8,128)(2,1)} %collective-permute-done.11), channel_id=1, source_target_pairs={{0,1},{1,0},{2,3},{3,2},{4,5},{5,4},{6,7},{7,6},{8,9},{9,8},{10,11... | collective-permute-start | bytes 786440 | tf_op jit(solution)/shard_map/ppermute | solution.py:471
  126.4 46.8 %copy-start = (s32[2048]{0:T(1024)S(1)}, s32[2048]{0:T(1024)}, u32[]{:S(2)}) copy-start(s32[2048]{0:T(1024)} %zs.1) | copy-start | bytes 24580
  126.5 46.8 %copy-start.1 = (s32[3]{0:T(128)S(1)}, s32[3]{0:T(128)}, u32[]{:S(2)}) copy-start(s32[3]{0:T(128)} %pad_add_fusion.sc) | copy-start | bytes 40
  169.2 4.0 %collective-permute-start.14 = (bf16[2048,256]{1,0:T(8,128)(2,1)S(1)}, bf16[2048,256]{1,0:T(8,128)(2,1)S(1)}, u32[]{:S(2)}, u32[]{:S(2)}) collective-permute-start(bf16[2048,256]{1,0:T(8,128)(2,1)S(1)} %bitcast.26), channel_id=1, source_target_pairs={{0,1},{1,0},{2,3},{3,2},{4,5},{5,4},{6,7},{7,6},{8,9},{9,8},{10,11... | collective-permute-start | bytes 3145736 | tf_op jit(solution)/shard_map/ppermute | solution.py:471
